TPU v7x, 256 devices: a whole 4x4x8 slice. The times are simulated.
256 devices in a mesh: pair: 2 (over x_hi), rows: 64 (over z, y, x_lo), cols: 2 (over core).
Axes of the slice: x: 4 (x_hi: 2, x_lo: 2; x = x_hi * 2 + x_lo), y: 4, z: 8, core: 2. Of those that a mesh axis runs over, the one named last changes fastest.
Arguments:
- source_image: bfloat16 [512, 512], P('rows', 'cols'), may hold values from -6 to 6
- target_images: bfloat16 [4, 512, 512], P('pair', 'rows', 'cols'), may hold values from -6 to 6
- prior_fields: float32 [4, 2, 512, 512], P('pair', None, 'rows', 'cols'), may hold values from -3 to 3
- offsets: int32 [4], P('pair'), may hold values from 0 to 2
- shift_lookup_matrix: bfloat16 [3, 128], replicated, may hold values from -6 to 6
- in_weight: bfloat16 [9, 2, 128], replicated, may hold values from -1.5 to 1.5
- in_bias: float32 [128], replicated, may hold values from -3 to 3
- hidden_weight: bfloat16 [2, 9, 128, 128], replicated, may hold values from -0.25 to 0.25
- hidden_bias: float32 [2, 128], replicated, may hold values from -2 to 2
- out_weight: bfloat16 [9, 2, 128], replicated, may hold values from -0.25 to 0.25
- out_bias: float32 [2], replicated, may hold values from -2 to 2
Outputs:
- candidates: float32 [4, 2, 512, 512], P('pair', None, 'rows', 'cols')
- voted: float32 [2, 512, 512], P(None, 'rows', 'cols')
All inputs are finite; a program needn't handle non-finite values.
Results may differ from a plain program's by a relative error of at most 0.0084.
Values may be sent and summed in bfloat16 or wider, within the bound.
A program may use at most 64 MiB of HBM per device.

v0:
```python
import jax
import jax.numpy as jnp
from jax import lax
from jax.sharding import PartitionSpec as P

smoothing_sharpness = 4.0
max_shift = 2.0


def extended(block, sides, width):
    for axis, dim in sides:
        count = lax.axis_size(axis)
        forward = [(i, i + 1) for i in range(count - 1)]
        backward = [(target, source) for source, target in forward]
        low = lax.ppermute(
            lax.slice_in_dim(block, block.shape[dim] - width, None, axis=dim), axis, forward
        )
        high = lax.ppermute(lax.slice_in_dim(block, 0, width, axis=dim), axis, backward)
        block = jnp.concatenate([low, block, high], axis=dim)
    return block


def conv_input(padded, weight):
    rows_out = padded.shape[2] - 2
    cols_out = padded.shape[3] - 2
    total = jnp.zeros((padded.shape[0], rows_out, cols_out, weight.shape[2]), jnp.float32)
    for position in range(9):
        window = padded[
            :, :, position // 3 : position // 3 + rows_out, position % 3 : position % 3 + cols_out
        ]
        total = total + jnp.einsum(
            "kerw,ed->krwd", window, weight[position], preferred_element_type=jnp.float32
        )
    return total


def conv_hidden(padded, weight, offset_term):
    rows_out = padded.shape[1] - 2
    cols_out = padded.shape[2] - 2
    total = jnp.zeros((padded.shape[0], rows_out, cols_out, weight.shape[2]), jnp.float32)
    for position in range(9):
        window = padded[
            :, position // 3 : position // 3 + rows_out, position % 3 : position % 3 + cols_out, :
        ]
        total = total + jnp.einsum(
            "krwc,cd->krwd", window, weight[position], preferred_element_type=jnp.float32
        )
    return total + offset_term


def conv_output(padded, weight):
    rows_out = padded.shape[1] - 2
    cols_out = padded.shape[2] - 2
    total = jnp.zeros((padded.shape[0], 2, rows_out, cols_out), jnp.float32)
    for position in range(9):
        window = padded[
            :, position // 3 : position // 3 + rows_out, position % 3 : position % 3 + cols_out, :
        ]
        total = total + jnp.einsum(
            "krwc,ec->kerw", window, weight[position], preferred_element_type=jnp.float32
        )
    return total


def pair_stack(bordered_images):
    targets = bordered_images[1:]
    source = jnp.broadcast_to(bordered_images[0], targets.shape)
    return jnp.stack([source, targets], axis=1)


def feature_rim(hidden):
    return extended(hidden, (("rows", 1), ("cols", 2)), 1)


def sample_window(prior_padded, row_pos, col_pos, row_base, col_base, tile_rows, tile_cols):
    col_weights = [
        jax.nn.relu(1.0 - jnp.abs(col_pos - (col_base + float(step))))[:, None]
        for step in range(-2, 4)
    ]
    total = jnp.zeros((prior_padded.shape[0], 2, tile_rows, tile_cols), jnp.float32)
    for row_step in range(-2, 4):
        row_weight = jax.nn.relu(1.0 - jnp.abs(row_pos - (row_base + float(row_step))))[:, None]
        band = prior_padded[:, :, row_step + 3 : row_step + 3 + tile_rows, :]
        inner = jnp.zeros_like(total)
        for index, col_step in enumerate(range(-2, 4)):
            inner = (
                inner + col_weights[index] * band[:, :, :, col_step + 3 : col_step + 3 + tile_cols]
            )
        total = total + row_weight * inner
    return total


def elect_consensus_flows(cands):
    number_of_flows = cands.shape[0]
    differ = cands[:, None] - cands[None, :]
    mutual_separation = jnp.sum(differ * differ, axis=2)
    ballot_weighting = jnp.sum(mutual_separation, axis=1) / (
        (number_of_flows - 1) * smoothing_sharpness
    )
    expo = jnp.exp(-ballot_weighting)
    weight = expo / jnp.sum(expo, axis=0)
    return jnp.sum(weight[:, None] * cands, axis=0)


def shards(
    source_image,
    target_images,
    prior_fields,
    offsets,
    shift_lookup_matrix,
    in_weight,
    in_bias,
    hidden_weight,
    hidden_bias,
    out_weight,
    out_bias,
):
    tile_rows, tile_cols = source_image.shape
    network_layers = hidden_weight.shape[0]
    images = jnp.concatenate([source_image[None], target_images], axis=0)
    chooser = (offsets[:, None] == jnp.arange(shift_lookup_matrix.shape[0])[None, :]).astype(
        jnp.bfloat16
    )
    embed = jnp.dot(chooser, shift_lookup_matrix, preferred_element_type=jnp.float32)
    bordered_images = extended(images, (("rows", 1), ("cols", 2)), 1)
    first = conv_input(pair_stack(bordered_images), in_weight) + in_bias + embed[:, None, None, :]
    hidden = jax.nn.relu(first).astype(jnp.bfloat16)
    for layer in range(network_layers):
        padded = feature_rim(hidden)
        hidden = jax.nn.relu(conv_hidden(padded, hidden_weight[layer], hidden_bias[layer])).astype(
            jnp.bfloat16
        )
    padded = feature_rim(hidden)
    flow_field = max_shift * jnp.tanh(conv_output(padded, out_weight) + out_bias[:, None, None])
    prior_padded = extended(prior_fields, (("rows", 2), ("cols", 3)), 3)
    row_start = lax.axis_index("rows") * tile_rows
    col_start = lax.axis_index("cols") * tile_cols
    row_base = (row_start + jnp.arange(tile_rows)).astype(jnp.float32)[None, :, None]
    col_base = (col_start + jnp.arange(tile_cols)).astype(jnp.float32)[None, None, :]
    row_pos = row_base + flow_field[:, 0]
    col_pos = col_base + flow_field[:, 1]
    sampled = sample_window(
        prior_padded, row_pos, col_pos, row_base, col_base, tile_rows, tile_cols
    )
    candidates = flow_field + sampled
    every = lax.all_gather(candidates, "pair", axis=0, tiled=True)
    voted = elect_consensus_flows(every)
    return (candidates, voted)


def solution(mesh):
    in_specs = (
        P("rows", "cols"),
        P("pair", "rows", "cols"),
        P("pair", None, "rows", "cols"),
        P("pair"),
        P(),
        P(),
        P(),
        P(),
        P(),
        P(),
        P(),
    )
    out_specs = (P("pair", None, "rows", "cols"), P(None, "rows", "cols"))
    return jax.shard_map(shards, mesh=mesh, in_specs=in_specs, out_specs=out_specs, check_vma=False)
```

profile of v0, /device:TPU:126, one launch (start us, length us, event | category | flops | bytes accessed | tf_op | source)
XLA Modules:
  0.0 118.1 jit_solution(10909422958748261199)
XLA Ops:
  0.7 0.8 pad_maximum_fusion.24
  1.4 5.0 %collective-permute-start = (bf16[3,1,256]{2,1,0:T(2,128)(2,1)S(1)}, bf16[3,1,256]{2,1,0:T(2,128)(2,1)S(1)}, u32[]{:S(2)}, u32[]{:S(2)}) collective-permute-start(bf16[3,1,256]{2,1,0:T(2,128)(2,1)S(1)} %get-tuple-element.50), channel_id=1, source_target_pairs={{0,2},{2,4},{4,6},{6,8},{8,10},{10,12},{12,14},{14,16},{16,18},{18... | collective-permute-start | bytes 4616 | tf_op jit(solution)/shard_map/ppermute | solution.py:15
  6.4 1.9 %collective-permute-start.1 = (bf16[3,1,256]{2,1,0:T(2,128)(2,1)S(1)}, bf16[3,1,256]{2,1,0:T(2,128)(2,1)S(1)}, u32[]{:S(2)}, u32[]{:S(2)}) collective-permute-start(bf16[3,1,256]{2,1,0:T(2,128)(2,1)S(1)} %get-tuple-element.51), channel_id=1, source_target_pairs={{2,0},{4,2},{6,4},{8,6},{10,8},{12,10},{14,12},{16,14},{18,16},{20... | collective-permute-start | bytes 4616 | tf_op jit(solution)/shard_map/ppermute | solution.py:18
  8.3 0.8 fusion.260
  9.2 8.1 %collective-permute-start.16 = (f32[2,2,3,256]{3,2,1,0:T(4,128)S(1)}, f32[2,2,3,256]{3,2,1,0:T(4,128)S(1)}, u32[]{:S(2)}, u32[]{:S(2)}) collective-permute-start(f32[2,2,3,256]{3,2,1,0:T(4,128)S(1)} %get-tuple-element.47), channel_id=1, source_target_pairs={{0,2},{2,4},{4,6},{6,8},{8,10},{10,12},{12,14},{14,16},{16,18},{18... | collective-permute-start | bytes 36872 | tf_op jit(solution)/shard_map/ppermute | solution.py:15
  17.3 1.9 %collective-permute-start.17 = (f32[2,2,3,256]{3,2,1,0:T(4,128)S(1)}, f32[2,2,3,256]{3,2,1,0:T(4,128)S(1)}, u32[]{:S(2)}, u32[]{:S(2)}) collective-permute-start(f32[2,2,3,256]{3,2,1,0:T(4,128)S(1)} %get-tuple-element.46), channel_id=1, source_target_pairs={{2,0},{4,2},{6,4},{8,6},{10,8},{12,10},{14,12},{16,14},{18,16},{20... | collective-permute-start | bytes 36872 | tf_op jit(solution)/shard_map/ppermute | solution.py:18
  19.3 0.8 constant_dynamic-update-slice_fusion.1
  20.1 0.8 slice_bitcast_fusion
  20.9 0.8 fusion.187
  21.7 0.7 pad_maximum_fusion.11
  22.5 1.3 %collective-permute-start.2 = (bf16[3,10,1]{2,1,0:T(8,128)(2,1)S(1)}, bf16[3,10,1]{2,1,0:T(8,128)(2,1)S(1)}, u32[]{:S(2)}, u32[]{:S(2)}) collective-permute-start(bf16[3,10,1]{2,1,0:T(8,128)(2,1)S(1)} %get-tuple-element.48), channel_id=1, source_target_pairs={{0,1},{2,3},{4,5},{6,7},{8,9},{10,11},{12,13},{14,15},{16,17},{18,... | collective-permute-start | bytes 188 | tf_op jit(solution)/shard_map/ppermute | solution.py:15
  23.8 1.3 %collective-permute-start.3 = (bf16[3,10,1]{2,1,0:T(8,128)(2,1)S(1)}, bf16[3,10,1]{2,1,0:T(8,128)(2,1)S(1)}, u32[]{:S(2)}, u32[]{:S(2)}) collective-permute-start(bf16[3,10,1]{2,1,0:T(8,128)(2,1)S(1)} %get-tuple-element.49), channel_id=1, source_target_pairs={{1,0},{3,2},{5,4},{7,6},{9,8},{11,10},{13,12},{15,14},{17,16},{19,... | collective-permute-start | bytes 188 | tf_op jit(solution)/shard_map/ppermute | solution.py:18
  25.1 1.8 %collective-permute-done.3 = bf16[3,10,1]{2,1,0:T(8,128)(2,1)S(1)} collective-permute-done((bf16[3,10,1]{2,1,0:T(8,128)(2,1)S(1)}, bf16[3,10,1]{2,1,0:T(8,128)(2,1)S(1)}, u32[]{:S(2)}, u32[]{:S(2)}) %collective-permute-start.3) | collective-permute-done | bytes 92 | tf_op jit(solution)/shard_map/ppermute | solution.py:18
  26.9 0.8 fusion.153
  27.7 0.8 maximum_bitcast_fusion.12
  28.5 1.2 %fusion.162 = f32[2,8,256,128]{3,2,1,0:T(8,128)S(1)} fusion(bf16[2,1,10,258]{3,1,2,0:T(2,128)(2,1)S(1)} %stack_broadcast_in_dim.3, bf16[9,2,128]{2,1,0:T(2,128)(2,1)} %param.16, bf16[2,1,10,258]{3,1,2,0:T(2,128)(2,1)S(1)} %copy.58), kind=kOutput, calls=%fused_computation.231 | convolution fusion | flops 2129920 | bytes 2118304 | tf_op jit(solution)/shard_map/kerw,ed->krwd/dot_general | solution.py:31
  29.7 1.0 fusion.164
  30.7 1.0 fusion.166
  31.8 0.5 fusion.168
  32.3 1.0 fusion.170
  33.3 1.0 fusion.172
  34.4 0.5 fusion.174
  34.9 1.0 fusion.176
  36.0 1.3 %maximum_convert_fusion.2 = bf16[2,8,256,128]{3,2,1,0:T(8,128)(2,1)S(1)} fusion(f32[2,8,256,128]{3,2,1,0:T(8,128)S(1)} %fusion.176, f32[2,8,256,128]{3,2,1,0:T(8,128)S(1)} %fusion.162, f32[2,8,256,128]{3,2,1,0:T(8,128)S(1)} %fusion.164, f32[2,8,256,128]{3,2,1,0:T(8,128)S(1)} %fusion.166, f32[2,8,256,128]{3,2,1,0:T(8,128)S(1)} %fusion.168, ...), kind=kOutput, calls=%fused_computation.2 | convolution fusion | flops 8421376 | bytes 17889280 | tf_op jit(solution)/shard_map/kerw,ed->krwd/dot_general | solution.py:31
  37.3 8.1 %collective-permute-start.4 = (bf16[2,1,256,128]{3,2,1,0:T(8,128)(2,1)S(1)}, bf16[2,1,256,128]{3,2,1,0:T(8,128)(2,1)S(1)}, u32[]{:S(2)}, u32[]{:S(2)}) collective-permute-start(bf16[2,1,256,128]{3,2,1,0:T(8,128)(2,1)S(1)} %get-tuple-element.28), channel_id=1, source_target_pairs={{0,2},{2,4},{4,6},{6,8},{8,10},{10,12},{12,14},{14,16},{16,18},{18... | collective-permute-start | bytes 393224 | tf_op jit(solution)/shard_map/ppermute | solution.py:15
  45.4 1.9 %collective-permute-start.5 = (bf16[2,1,256,128]{3,2,1,0:T(8,128)(2,1)S(1)}, bf16[2,1,256,128]{3,2,1,0:T(8,128)(2,1)S(1)}, u32[]{:S(2)}, u32[]{:S(2)}) collective-permute-start(bf16[2,1,256,128]{3,2,1,0:T(8,128)(2,1)S(1)} %get-tuple-element.29), channel_id=1, source_target_pairs={{2,0},{4,2},{6,4},{8,6},{10,8},{12,10},{14,12},{16,14},{18,16},{20... | collective-permute-start | bytes 393224 | tf_op jit(solution)/shard_map/ppermute | solution.py:18
  47.3 0.4 fusion.123
  47.9 1.8 %collective-permute-start.18 = (f32[2,2,14,3]{3,2,1,0:T(8,128)S(1)}, f32[2,2,14,3]{3,2,1,0:T(8,128)S(1)}, u32[]{:S(2)}, u32[]{:S(2)}) collective-permute-start(f32[2,2,14,3]{3,2,1,0:T(8,128)S(1)} %get-tuple-element.32), channel_id=1, source_target_pairs={{0,1},{2,3},{4,5},{6,7},{8,9},{10,11},{12,13},{14,15},{16,17},{18,... | collective-permute-start | bytes 2024 | tf_op jit(solution)/shard_map/ppermute | solution.py:15
  49.7 1.3 %collective-permute-start.19 = (f32[2,2,14,3]{3,2,1,0:T(8,128)S(1)}, f32[2,2,14,3]{3,2,1,0:T(8,128)S(1)}, u32[]{:S(2)}, u32[]{:S(2)}) collective-permute-start(f32[2,2,14,3]{3,2,1,0:T(8,128)S(1)} %get-tuple-element.33), channel_id=1, source_target_pairs={{1,0},{3,2},{5,4},{7,6},{9,8},{11,10},{13,12},{15,14},{17,16},{19,... | collective-permute-start | bytes 2024 | tf_op jit(solution)/shard_map/ppermute | solution.py:18
  51.0 1.8 %collective-permute-done.19 = f32[2,2,14,3]{3,2,1,0:T(8,128)S(1)} collective-permute-done((f32[2,2,14,3]{3,2,1,0:T(8,128)S(1)}, f32[2,2,14,3]{3,2,1,0:T(8,128)S(1)}, u32[]{:S(2)}, u32[]{:S(2)}) %collective-permute-start.19) | collective-permute-done | bytes 704 | tf_op jit(solution)/shard_map/ppermute | solution.py:18
  52.9 3.9 %collective-permute-done.5 = bf16[2,1,256,128]{3,2,1,0:T(8,128)(2,1)S(1)} collective-permute-done((bf16[2,1,256,128]{3,2,1,0:T(8,128)(2,1)S(1)}, bf16[2,1,256,128]{3,2,1,0:T(8,128)(2,1)S(1)}, u32[]{:S(2)}, u32[]{:S(2)}) %collective-permute-start.5) | collective-permute-done | bytes 131104 | tf_op jit(solution)/shard_map/ppermute | solution.py:18
  56.8 1.3 %collective-permute-start.6 = (bf16[2,10,1,128]{3,2,1,0:T(2,128)(2,1)S(1)}, bf16[2,10,1,128]{3,2,1,0:T(2,128)(2,1)S(1)}, u32[]{:S(2)}, u32[]{:S(2)}) collective-permute-start(bf16[2,10,1,128]{3,2,1,0:T(2,128)(2,1)S(1)} %get-tuple-element.23), channel_id=1, source_target_pairs={{0,1},{2,3},{4,5},{6,7},{8,9},{10,11},{12,13},{14,15},{16,17},{18,... | collective-permute-start | bytes 15368 | tf_op jit(solution)/shard_map/ppermute | solution.py:15
  58.1 1.3 %collective-permute-start.7 = (bf16[2,10,1,128]{3,2,1,0:T(2,128)(2,1)S(1)}, bf16[2,10,1,128]{3,2,1,0:T(2,128)(2,1)S(1)}, u32[]{:S(2)}, u32[]{:S(2)}) collective-permute-start(bf16[2,10,1,128]{3,2,1,0:T(2,128)(2,1)S(1)} %get-tuple-element.22), channel_id=1, source_target_pairs={{1,0},{3,2},{5,4},{7,6},{9,8},{11,10},{13,12},{15,14},{17,16},{19,... | collective-permute-start | bytes 15368 | tf_op jit(solution)/shard_map/ppermute | solution.py:18
  59.8 0.4 fusion.4
  60.3 0.9 collective-permute-done.7
  61.2 0.5 pad_maximum_fusion
  62.5 0.4 fusion.56
  63.0 0.4 fusion.60
  63.8 1.2 maximum_convert_fusion.1
  65.0 4.8 %collective-permute-start.8 = (bf16[2,1,256,128]{3,2,1,0:T(8,128)(2,1)S(1)}, bf16[2,1,256,128]{3,2,1,0:T(8,128)(2,1)S(1)}, u32[]{:S(2)}, u32[]{:S(2)}) collective-permute-start(bf16[2,1,256,128]{3,2,1,0:T(8,128)(2,1)S(1)} %get-tuple-element.26), channel_id=1, source_target_pairs={{0,2},{2,4},{4,6},{6,8},{8,10},{10,12},{12,14},{14,16},{16,18},{18... | collective-permute-start | bytes 393224 | tf_op jit(solution)/shard_map/ppermute | solution.py:15
  69.8 1.9 %collective-permute-start.9 = (bf16[2,1,256,128]{3,2,1,0:T(8,128)(2,1)S(1)}, bf16[2,1,256,128]{3,2,1,0:T(8,128)(2,1)S(1)}, u32[]{:S(2)}, u32[]{:S(2)}) collective-permute-start(bf16[2,1,256,128]{3,2,1,0:T(8,128)(2,1)S(1)} %get-tuple-element.27), channel_id=1, source_target_pairs={{2,0},{4,2},{6,4},{8,6},{10,8},{12,10},{14,12},{16,14},{18,16},{20... | collective-permute-start | bytes 393224 | tf_op jit(solution)/shard_map/ppermute | solution.py:18
  72.1 1.1 collective-permute-done.8
  73.2 8.0 %collective-permute-done.9 = bf16[2,1,256,128]{3,2,1,0:T(8,128)(2,1)S(1)} collective-permute-done((bf16[2,1,256,128]{3,2,1,0:T(8,128)(2,1)S(1)}, bf16[2,1,256,128]{3,2,1,0:T(8,128)(2,1)S(1)}, u32[]{:S(2)}, u32[]{:S(2)}) %collective-permute-start.9) | collective-permute-done | bytes 131104 | tf_op jit(solution)/shard_map/ppermute | solution.py:18
  81.3 1.3 %collective-permute-start.10 = (bf16[2,10,1,128]{3,2,1,0:T(2,128)(2,1)S(1)}, bf16[2,10,1,128]{3,2,1,0:T(2,128)(2,1)S(1)}, u32[]{:S(2)}, u32[]{:S(2)}) collective-permute-start(bf16[2,10,1,128]{3,2,1,0:T(2,128)(2,1)S(1)} %get-tuple-element.19), channel_id=1, source_target_pairs={{0,1},{2,3},{4,5},{6,7},{8,9},{10,11},{12,13},{14,15},{16,17},{18,... | collective-permute-start | bytes 15368 | tf_op jit(solution)/shard_map/ppermute | solution.py:15
  82.6 1.5 %collective-permute-start.11 = (bf16[2,10,1,128]{3,2,1,0:T(2,128)(2,1)S(1)}, bf16[2,10,1,128]{3,2,1,0:T(2,128)(2,1)S(1)}, u32[]{:S(2)}, u32[]{:S(2)}) collective-permute-start(bf16[2,10,1,128]{3,2,1,0:T(2,128)(2,1)S(1)} %get-tuple-element.18), channel_id=1, source_target_pairs={{1,0},{3,2},{5,4},{7,6},{9,8},{11,10},{13,12},{15,14},{17,16},{19,... | collective-permute-start | bytes 15368 | tf_op jit(solution)/shard_map/ppermute | solution.py:18
  84.1 0.4 fusion.8
  84.5 0.4 fusion.12
  84.9 0.7 collective-permute-done.11
  85.6 0.5 pad_maximum_fusion.1
  86.1 0.4 fusion.40
  86.6 0.4 fusion.44
  87.0 0.4 fusion.42
  87.4 0.4 fusion.46
  88.3 1.1 maximum_convert_fusion
  89.5 1.9 %collective-permute-start.12 = (bf16[2,1,256,128]{3,2,1,0:T(8,128)(2,1)S(1)}, bf16[2,1,256,128]{3,2,1,0:T(8,128)(2,1)S(1)}, u32[]{:S(2)}, u32[]{:S(2)}) collective-permute-start(bf16[2,1,256,128]{3,2,1,0:T(8,128)(2,1)S(1)} %get-tuple-element.24), channel_id=1, source_target_pairs={{0,2},{2,4},{4,6},{6,8},{8,10},{10,12},{12,14},{14,16},{16,18},{18... | collective-permute-start | bytes 393224 | tf_op jit(solution)/shard_map/ppermute | solution.py:15
  91.4 4.0 %collective-permute-start.13 = (bf16[2,1,256,128]{3,2,1,0:T(8,128)(2,1)S(1)}, bf16[2,1,256,128]{3,2,1,0:T(8,128)(2,1)S(1)}, u32[]{:S(2)}, u32[]{:S(2)}) collective-permute-start(bf16[2,1,256,128]{3,2,1,0:T(8,128)(2,1)S(1)} %get-tuple-element.25), channel_id=1, source_target_pairs={{2,0},{4,2},{6,4},{8,6},{10,8},{12,10},{14,12},{16,14},{18,16},{20... | collective-permute-start | bytes 393224 | tf_op jit(solution)/shard_map/ppermute | solution.py:18
  95.7 2.0 %collective-permute-done.12 = bf16[2,1,256,128]{3,2,1,0:T(8,128)(2,1)S(1)} collective-permute-done((bf16[2,1,256,128]{3,2,1,0:T(8,128)(2,1)S(1)}, bf16[2,1,256,128]{3,2,1,0:T(8,128)(2,1)S(1)}, u32[]{:S(2)}, u32[]{:S(2)}) %collective-permute-start.12) | collective-permute-done | bytes 131104 | tf_op jit(solution)/shard_map/ppermute | solution.py:15
  97.7 5.6 %collective-permute-done.13 = bf16[2,1,256,128]{3,2,1,0:T(8,128)(2,1)S(1)} collective-permute-done((bf16[2,1,256,128]{3,2,1,0:T(8,128)(2,1)S(1)}, bf16[2,1,256,128]{3,2,1,0:T(8,128)(2,1)S(1)}, u32[]{:S(2)}, u32[]{:S(2)}) %collective-permute-start.13) | collective-permute-done | bytes 131104 | tf_op jit(solution)/shard_map/ppermute | solution.py:18
  103.3 1.5 %collective-permute-start.14 = (bf16[2,10,1,128]{3,2,1,0:T(2,128)(2,1)S(1)}, bf16[2,10,1,128]{3,2,1,0:T(2,128)(2,1)S(1)}, u32[]{:S(2)}, u32[]{:S(2)}) collective-permute-start(bf16[2,10,1,128]{3,2,1,0:T(2,128)(2,1)S(1)} %get-tuple-element.14), channel_id=1, source_target_pairs={{0,1},{2,3},{4,5},{6,7},{8,9},{10,11},{12,13},{14,15},{16,17},{18,... | collective-permute-start | bytes 15368 | tf_op jit(solution)/shard_map/ppermute | solution.py:15
  104.8 1.3 %collective-permute-start.15 = (bf16[2,10,1,128]{3,2,1,0:T(2,128)(2,1)S(1)}, bf16[2,10,1,128]{3,2,1,0:T(2,128)(2,1)S(1)}, u32[]{:S(2)}, u32[]{:S(2)}) collective-permute-start(bf16[2,10,1,128]{3,2,1,0:T(2,128)(2,1)S(1)} %get-tuple-element.15), channel_id=1, source_target_pairs={{1,0},{3,2},{5,4},{7,6},{9,8},{11,10},{13,12},{15,14},{17,16},{19,... | collective-permute-start | bytes 15368 | tf_op jit(solution)/shard_map/ppermute | solution.py:18
  106.9 1.0 collective-permute-done.15
  107.9 0.5 maximum_maximum_fusion.2
  111.3 6.1 %all_gather.3 = f32[4,2,8,256]{3,2,1,0:T(8,128)S(1)} all-gather(f32[2,2,8,256]{3,2,1,0:T(8,128)S(1)} %fusion.76), channel_id=1, replica_groups=mesh['pair'=2,'rows'=64,'cols'=2] {'pair'}, dimensions={0}, use_global_device_ids=true | all-gather | bytes 98304 | tf_op jit(solution)/shard_map/all_gather | solution.py:146
  117.5 0.6 multiply_reduce_fusion.1
  (69 shorter events, 7.1 us)
Async XLA Ops:
  0.6 20.2 %copy-start = (bf16[3,128]{1,0:T(4,128)(2,1)S(1)}, bf16[3,128]{1,0:T(4,128)(2,1)}, u32[]{:S(2)}) copy-start(bf16[3,128]{1,0:T(4,128)(2,1)} %param.15) | copy-start | bytes 2308
  0.6 29.1 %copy-start.4 = (bf16[9,2,128]{2,1,0:T(2,128)(2,1)S(1)}, bf16[9,2,128]{2,1,0:T(2,128)(2,1)}, u32[]{:S(2)}) copy-start(bf16[9,2,128]{2,1,0:T(2,128)(2,1)} %param.16) | copy-start | bytes 13828
  1.4 20.3 %collective-permute-start = (bf16[3,1,256]{2,1,0:T(2,128)(2,1)S(1)}, bf16[3,1,256]{2,1,0:T(2,128)(2,1)S(1)}, u32[]{:S(2)}, u32[]{:S(2)}) collective-permute-start(bf16[3,1,256]{2,1,0:T(2,128)(2,1)S(1)} %get-tuple-element.50), channel_id=1, source_target_pairs={{0,2},{2,4},{4,6},{6,8},{8,10},{10,12},{12,14},{14,16},{16,18},{18... | collective-permute-start | bytes 4616 | tf_op jit(solution)/shard_map/ppermute | solution.py:15
  6.4 15.3 %collective-permute-start.1 = (bf16[3,1,256]{2,1,0:T(2,128)(2,1)S(1)}, bf16[3,1,256]{2,1,0:T(2,128)(2,1)S(1)}, u32[]{:S(2)}, u32[]{:S(2)}) collective-permute-start(bf16[3,1,256]{2,1,0:T(2,128)(2,1)S(1)} %get-tuple-element.51), channel_id=1, source_target_pairs={{2,0},{4,2},{6,4},{8,6},{10,8},{12,10},{14,12},{16,14},{18,16},{20... | collective-permute-start | bytes 4616 | tf_op jit(solution)/shard_map/ppermute | solution.py:18
  9.2 38.6 %collective-permute-start.16 = (f32[2,2,3,256]{3,2,1,0:T(4,128)S(1)}, f32[2,2,3,256]{3,2,1,0:T(4,128)S(1)}, u32[]{:S(2)}, u32[]{:S(2)}) collective-permute-start(f32[2,2,3,256]{3,2,1,0:T(4,128)S(1)} %get-tuple-element.47), channel_id=1, source_target_pairs={{0,2},{2,4},{4,6},{6,8},{8,10},{10,12},{12,14},{14,16},{16,18},{18... | collective-permute-start | bytes 36872 | tf_op jit(solution)/shard_map/ppermute | solution.py:15
  17.3 30.5 %collective-permute-start.17 = (f32[2,2,3,256]{3,2,1,0:T(4,128)S(1)}, f32[2,2,3,256]{3,2,1,0:T(4,128)S(1)}, u32[]{:S(2)}, u32[]{:S(2)}) collective-permute-start(f32[2,2,3,256]{3,2,1,0:T(4,128)S(1)} %get-tuple-element.46), channel_id=1, source_target_pairs={{2,0},{4,2},{6,4},{8,6},{10,8},{12,10},{14,12},{16,14},{18,16},{20... | collective-permute-start | bytes 36872 | tf_op jit(solution)/shard_map/ppermute | solution.py:18
  22.5 2.6 %collective-permute-start.2 = (bf16[3,10,1]{2,1,0:T(8,128)(2,1)S(1)}, bf16[3,10,1]{2,1,0:T(8,128)(2,1)S(1)}, u32[]{:S(2)}, u32[]{:S(2)}) collective-permute-start(bf16[3,10,1]{2,1,0:T(8,128)(2,1)S(1)} %get-tuple-element.48), channel_id=1, source_target_pairs={{0,1},{2,3},{4,5},{6,7},{8,9},{10,11},{12,13},{14,15},{16,17},{18,... | collective-permute-start | bytes 188 | tf_op jit(solution)/shard_map/ppermute | solution.py:15
  23.8 3.1 %collective-permute-start.3 = (bf16[3,10,1]{2,1,0:T(8,128)(2,1)S(1)}, bf16[3,10,1]{2,1,0:T(8,128)(2,1)S(1)}, u32[]{:S(2)}, u32[]{:S(2)}) collective-permute-start(bf16[3,10,1]{2,1,0:T(8,128)(2,1)S(1)} %get-tuple-element.49), channel_id=1, source_target_pairs={{1,0},{3,2},{5,4},{7,6},{9,8},{11,10},{13,12},{15,14},{17,16},{19,... | collective-permute-start | bytes 188 | tf_op jit(solution)/shard_map/ppermute | solution.py:18
  34.4 1.6 %copy-start.5 = (f32[128]{0:T(128)S(1)}, f32[128]{0:T(128)}, u32[]{:S(2)}) copy-start(f32[128]{0:T(128)} %param.17) | copy-start | bytes 1540
  35.9 11.4 %copy-start.2 = (bf16[2,9,128,128]{3,2,1,0:T(8,128)(2,1)S(1)}, bf16[2,9,128,128]{3,2,1,0:T(8,128)(2,1)}, u32[]{:S(2)}) copy-start(bf16[2,9,128,128]{3,2,1,0:T(8,128)(2,1)} %param.18) | copy-start | bytes 1769476
  37.2 10.6 %copy-start.1 = (f32[2,2,8,256]{3,2,1,0:T(8,128)S(1)}, f32[2,2,8,256]{3,2,1,0:T(8,128)}, u32[]{:S(2)}) copy-start(f32[2,2,8,256]{3,2,1,0:T(8,128)} %param.13) | copy-start | bytes 98308
  37.3 15.6 %collective-permute-start.4 = (bf16[2,1,256,128]{3,2,1,0:T(8,128)(2,1)S(1)}, bf16[2,1,256,128]{3,2,1,0:T(8,128)(2,1)S(1)}, u32[]{:S(2)}, u32[]{:S(2)}) collective-permute-start(bf16[2,1,256,128]{3,2,1,0:T(8,128)(2,1)S(1)} %get-tuple-element.28), channel_id=1, source_target_pairs={{0,2},{2,4},{4,6},{6,8},{8,10},{10,12},{12,14},{14,16},{16,18},{18... | collective-permute-start | bytes 393224 | tf_op jit(solution)/shard_map/ppermute | solution.py:15
  45.4 11.4 %collective-permute-start.5 = (bf16[2,1,256,128]{3,2,1,0:T(8,128)(2,1)S(1)}, bf16[2,1,256,128]{3,2,1,0:T(8,128)(2,1)S(1)}, u32[]{:S(2)}, u32[]{:S(2)}) collective-permute-start(bf16[2,1,256,128]{3,2,1,0:T(8,128)(2,1)S(1)} %get-tuple-element.29), channel_id=1, source_target_pairs={{2,0},{4,2},{6,4},{8,6},{10,8},{12,10},{14,12},{16,14},{18,16},{20... | collective-permute-start | bytes 393224 | tf_op jit(solution)/shard_map/ppermute | solution.py:18
  47.9 3.1 %collective-permute-start.18 = (f32[2,2,14,3]{3,2,1,0:T(8,128)S(1)}, f32[2,2,14,3]{3,2,1,0:T(8,128)S(1)}, u32[]{:S(2)}, u32[]{:S(2)}) collective-permute-start(f32[2,2,14,3]{3,2,1,0:T(8,128)S(1)} %get-tuple-element.32), channel_id=1, source_target_pairs={{0,1},{2,3},{4,5},{6,7},{8,9},{10,11},{12,13},{14,15},{16,17},{18,... | collective-permute-start | bytes 2024 | tf_op jit(solution)/shard_map/ppermute | solution.py:15
  49.7 3.1 %collective-permute-start.19 = (f32[2,2,14,3]{3,2,1,0:T(8,128)S(1)}, f32[2,2,14,3]{3,2,1,0:T(8,128)S(1)}, u32[]{:S(2)}, u32[]{:S(2)}) collective-permute-start(f32[2,2,14,3]{3,2,1,0:T(8,128)S(1)} %get-tuple-element.33), channel_id=1, source_target_pairs={{1,0},{3,2},{5,4},{7,6},{9,8},{11,10},{13,12},{15,14},{17,16},{19,... | collective-permute-start | bytes 2024 | tf_op jit(solution)/shard_map/ppermute | solution.py:18
  56.8 3.4 %collective-permute-start.6 = (bf16[2,10,1,128]{3,2,1,0:T(2,128)(2,1)S(1)}, bf16[2,10,1,128]{3,2,1,0:T(2,128)(2,1)S(1)}, u32[]{:S(2)}, u32[]{:S(2)}) collective-permute-start(bf16[2,10,1,128]{3,2,1,0:T(2,128)(2,1)S(1)} %get-tuple-element.23), channel_id=1, source_target_pairs={{0,1},{2,3},{4,5},{6,7},{8,9},{10,11},{12,13},{14,15},{16,17},{18,... | collective-permute-start | bytes 15368 | tf_op jit(solution)/shard_map/ppermute | solution.py:15
  58.1 3.1 %collective-permute-start.7 = (bf16[2,10,1,128]{3,2,1,0:T(2,128)(2,1)S(1)}, bf16[2,10,1,128]{3,2,1,0:T(2,128)(2,1)S(1)}, u32[]{:S(2)}, u32[]{:S(2)}) collective-permute-start(bf16[2,10,1,128]{3,2,1,0:T(2,128)(2,1)S(1)} %get-tuple-element.22), channel_id=1, source_target_pairs={{1,0},{3,2},{5,4},{7,6},{9,8},{11,10},{13,12},{15,14},{17,16},{19,... | collective-permute-start | bytes 15368 | tf_op jit(solution)/shard_map/ppermute | solution.py:18
  65.0 8.2 %collective-permute-start.8 = (bf16[2,1,256,128]{3,2,1,0:T(8,128)(2,1)S(1)}, bf16[2,1,256,128]{3,2,1,0:T(8,128)(2,1)S(1)}, u32[]{:S(2)}, u32[]{:S(2)}) collective-permute-start(bf16[2,1,256,128]{3,2,1,0:T(8,128)(2,1)S(1)} %get-tuple-element.26), channel_id=1, source_target_pairs={{0,2},{2,4},{4,6},{6,8},{8,10},{10,12},{12,14},{14,16},{16,18},{18... | collective-permute-start | bytes 393224 | tf_op jit(solution)/shard_map/ppermute | solution.py:15
  69.8 11.5 %collective-permute-start.9 = (bf16[2,1,256,128]{3,2,1,0:T(8,128)(2,1)S(1)}, bf16[2,1,256,128]{3,2,1,0:T(8,128)(2,1)S(1)}, u32[]{:S(2)}, u32[]{:S(2)}) collective-permute-start(bf16[2,1,256,128]{3,2,1,0:T(8,128)(2,1)S(1)} %get-tuple-element.27), channel_id=1, source_target_pairs={{2,0},{4,2},{6,4},{8,6},{10,8},{12,10},{14,12},{16,14},{18,16},{20... | collective-permute-start | bytes 393224 | tf_op jit(solution)/shard_map/ppermute | solution.py:18
  81.3 3.6 %collective-permute-start.10 = (bf16[2,10,1,128]{3,2,1,0:T(2,128)(2,1)S(1)}, bf16[2,10,1,128]{3,2,1,0:T(2,128)(2,1)S(1)}, u32[]{:S(2)}, u32[]{:S(2)}) collective-permute-start(bf16[2,10,1,128]{3,2,1,0:T(2,128)(2,1)S(1)} %get-tuple-element.19), channel_id=1, source_target_pairs={{0,1},{2,3},{4,5},{6,7},{8,9},{10,11},{12,13},{14,15},{16,17},{18,... | collective-permute-start | bytes 15368 | tf_op jit(solution)/shard_map/ppermute | solution.py:15
  82.6 3.1 %collective-permute-start.11 = (bf16[2,10,1,128]{3,2,1,0:T(2,128)(2,1)S(1)}, bf16[2,10,1,128]{3,2,1,0:T(2,128)(2,1)S(1)}, u32[]{:S(2)}, u32[]{:S(2)}) collective-permute-start(bf16[2,10,1,128]{3,2,1,0:T(2,128)(2,1)S(1)} %get-tuple-element.18), channel_id=1, source_target_pairs={{1,0},{3,2},{5,4},{7,6},{9,8},{11,10},{13,12},{15,14},{17,16},{19,... | collective-permute-start | bytes 15368 | tf_op jit(solution)/shard_map/ppermute | solution.py:18
  88.3 7.1 %copy-start.7 = (bf16[9,2,128]{2,1,0:T(2,128)(2,1)S(1)}, bf16[9,2,128]{2,1,0:T(2,128)(2,1)}, u32[]{:S(2)}) copy-start(bf16[9,2,128]{2,1,0:T(2,128)(2,1)} %param.20) | copy-start | bytes 13828
  89.5 8.2 %collective-permute-start.12 = (bf16[2,1,256,128]{3,2,1,0:T(8,128)(2,1)S(1)}, bf16[2,1,256,128]{3,2,1,0:T(8,128)(2,1)S(1)}, u32[]{:S(2)}, u32[]{:S(2)}) collective-permute-start(bf16[2,1,256,128]{3,2,1,0:T(8,128)(2,1)S(1)} %get-tuple-element.24), channel_id=1, source_target_pairs={{0,2},{2,4},{4,6},{6,8},{8,10},{10,12},{12,14},{14,16},{16,18},{18... | collective-permute-start | bytes 393224 | tf_op jit(solution)/shard_map/ppermute | solution.py:15
  91.4 11.9 %collective-permute-start.13 = (bf16[2,1,256,128]{3,2,1,0:T(8,128)(2,1)S(1)}, bf16[2,1,256,128]{3,2,1,0:T(8,128)(2,1)S(1)}, u32[]{:S(2)}, u32[]{:S(2)}) collective-permute-start(bf16[2,1,256,128]{3,2,1,0:T(8,128)(2,1)S(1)} %get-tuple-element.25), channel_id=1, source_target_pairs={{2,0},{4,2},{6,4},{8,6},{10,8},{12,10},{14,12},{16,14},{18,16},{20... | collective-permute-start | bytes 393224 | tf_op jit(solution)/shard_map/ppermute | solution.py:18
  103.3 3.5 %collective-permute-start.14 = (bf16[2,10,1,128]{3,2,1,0:T(2,128)(2,1)S(1)}, bf16[2,10,1,128]{3,2,1,0:T(2,128)(2,1)S(1)}, u32[]{:S(2)}, u32[]{:S(2)}) collective-permute-start(bf16[2,10,1,128]{3,2,1,0:T(2,128)(2,1)S(1)} %get-tuple-element.14), channel_id=1, source_target_pairs={{0,1},{2,3},{4,5},{6,7},{8,9},{10,11},{12,13},{14,15},{16,17},{18,... | collective-permute-start | bytes 15368 | tf_op jit(solution)/shard_map/ppermute | solution.py:15
  104.8 3.1 %collective-permute-start.15 = (bf16[2,10,1,128]{3,2,1,0:T(2,128)(2,1)S(1)}, bf16[2,10,1,128]{3,2,1,0:T(2,128)(2,1)S(1)}, u32[]{:S(2)}, u32[]{:S(2)}) collective-permute-start(bf16[2,10,1,128]{3,2,1,0:T(2,128)(2,1)S(1)} %get-tuple-element.15), channel_id=1, source_target_pairs={{1,0},{3,2},{5,4},{7,6},{9,8},{11,10},{13,12},{15,14},{17,16},{19,... | collective-permute-start | bytes 15368 | tf_op jit(solution)/shard_map/ppermute | solution.py:18
  109.5 1.2 copy-start.6
  111.3 6.8 %copy-start.3 = (f32[2,2,8,256]{3,2,1,0:T(8,128)}, f32[2,2,8,256]{3,2,1,0:T(8,128)S(1)}, u32[]{:S(2)}) copy-start(f32[2,2,8,256]{3,2,1,0:T(8,128)S(1)} %fusion.76) | copy-start | bytes 98308
where the time goes:
time: 119 us; the launch traced here: 118 us
  starting transfers between devices  53.3 us (45%)
  waiting for transfers between devices  26.8 us (23%)
  matrix products  21.9 us (18%)
  blocking collectives  6.1 us (5%)
  other arithmetic  6.02 us (5%)
  local copies, waits for them, and re-layouts  2.68 us (2%)
  between operations  1.22 us (1%)
    ppermute x10, starting transfers between devices, extended(): lax.ppermute(lax.slice_in_dim(block, block.shape[dim] - width, None, axis...  35 us
    ppermute x10, waiting for transfers between devices, extended(): lax.ppermute(lax.slice_in_dim(block, 0, width, axis=dim), axis, backward)  23.7 us
    ppermute x10, starting transfers between devices, extended(): lax.ppermute(lax.slice_in_dim(block, 0, width, axis=dim), axis, backward)  18.3 us
    dot_general x18, matrix products, conv_hidden(): jnp.einsum('krwc,cd->krwd', window, weight[position], preferred_element_t...  9.02 us
    dot_general x9, matrix products, conv_input(): jnp.einsum('kerw,ed->krwd', window, weight[position], preferred_element_t...  8.66 us
    all_gather x1, blocking collectives, shards(): every = lax.all_gather(candidates, 'pair', axis=0, tiled=True)  6.1 us
    dot_general x9, matrix products, conv_output(): jnp.einsum('krwc,ec->kerw', window, weight[position], preferred_element_t...  3.43 us
    ppermute x10, waiting for transfers between devices, extended(): lax.ppermute(lax.slice_in_dim(block, block.shape[dim] - width, None, axis...  3.1 us
  transfers between devices with their start and end apart: 20, of which 10 were waited for; matrix products, arithmetic and copies ran while one was open for 15% of the time, Pallas kernels for 0%

commit v1 on v0

v1 whole, which is shorter than its diff:
```python
import functools

import jax
import jax.numpy as jnp
from jax import lax
from jax.experimental import pallas as pl
from jax.experimental.pallas import tpu as pltpu
from jax.sharding import PartitionSpec as P

MESH = pl.DeviceIdType.MESH
BF = jnp.bfloat16
F32 = jnp.float32

sharpness = 4.0
max_shift = 2.0
OFF = -1e30

Q = 16
STRIDE = 17
ROWS_M = STRIDE * Q
ROWS_X = (STRIDE + 2) * Q
RING = 384


def dot(a, b, dims=((1,), (0,))):
    return lax.dot_general(a, b, (dims, ((), ())), preferred_element_type=F32)


def store_slabs(ref, index, y):
    ref[index, 0:ROWS_M, :] = y.astype(BF)
    first = pltpu.roll(y[0:Q], Q - 1, 0)
    second = pltpu.roll(y[Q : 2 * Q], Q - 1, 0)
    ref[index, ROWS_M:ROWS_X, :] = jnp.concatenate([first, second], axis=0).astype(BF)


def kernel(
    n_rows,
    src_ref,
    tgt_ref,
    prior_ref,
    off_ref,
    table_ref,
    inw_ref,
    inb_ref,
    hw_ref,
    hb_ref,
    outw_ref,
    outb_ref,
    cand_ref,
    vote_ref,
    img,
    side,
    pri,
    wts,
    pmat,
    qmat,
    gin,
    toe,
    gout,
    wout,
    feat,
    hid1,
    hid2,
    masks,
    every,
    w_sem,
    p_sem,
    img_send,
    img_recv,
    pri_send,
    pri_recv,
    cand_send,
    cand_recv,
):
    pair = lax.axis_index("pair")
    row = lax.axis_index("rows")
    col = lax.axis_index("cols")
    up = lax.rem(row + n_rows - 1, n_rows)
    down = lax.rem(row + 1, n_rows)
    other = 1 - col
    partner = 1 - pair
    tile_rows = 8
    rows_all = n_rows * tile_rows
    places = (
        (pair, up, col),
        (pair, down, col),
        (pair, row, other),
        (pair, up, other),
        (pair, down, other),
    )

    barrier = pltpu.get_barrier_semaphore()
    for place in places + ((partner, row, col),):
        pl.semaphore_signal(barrier, inc=1, device_id=place, device_id_type=MESH)

    weight_copies = []
    for number, (a, where, r0, l0) in enumerate(
        ((0, 0, 0, 0), (1, 0, 128, 0), (0, 0, 128, 128), (2, 1, 0, 0), (1, 1, 0, 128), (2, 1, 128, 128))
    ):
        copy = pltpu.make_async_copy(
            hw_ref.at[:, pl.ds(3 * a, 3)],
            wts.at[:, :, where, pl.ds(r0, 128), pl.ds(l0, 128)],
            w_sem.at[number],
        )
        copy.start()
        weight_copies.append(copy)
    own_prior = pltpu.make_async_copy(
        prior_ref, pri.at[:, :, pl.ds(8, 8), pl.ds(0, 256)], p_sem
    )
    own_prior.start()

    src = src_ref[...].astype(F32)
    tgt = tgt_ref[...].astype(F32)
    own = jnp.concatenate([src, tgt[0], tgt[1], jnp.zeros_like(src)], axis=0).astype(BF)
    img[0, :, 0:256] = own
    side[...] = jnp.where(col == 0, own[:, 128:256], own[:, 0:128])

    pl.semaphore_wait(barrier, 6)

    main = pl.ds(0, 256)
    edge = pl.ds(256, 128)
    routes = ((2, main), (1, main), (0, edge), (2, edge), (1, edge))
    image_copies = []
    for number, (slot, lanes) in enumerate(routes):
        copy = pltpu.make_async_remote_copy(
            src_ref=img.at[0, :, main] if number < 2 else side,
            dst_ref=img.at[slot, :, lanes],
            send_sem=img_send.at[number],
            recv_sem=img_recv.at[number],
            device_id=places[number],
            device_id_type=MESH,
        )
        copy.start()
        image_copies.append(copy)
    half = pl.ds(pl.multiple_of((1 - col) * 128, 128), 128)
    prior_copies = []
    for number, (slot, lanes) in enumerate(routes):
        start = (8, 0, 16)[slot]
        copy = pltpu.make_async_remote_copy(
            src_ref=prior_ref if number < 2 else prior_ref.at[:, :, :, half],
            dst_ref=pri.at[:, :, pl.ds(start, 8), lanes],
            send_sem=pri_send.at[number],
            recv_sem=pri_recv.at[number],
            device_id=places[number],
            device_id_type=MESH,
        )
        copy.start()
        prior_copies.append(copy)

    slab = lax.broadcasted_iota(jnp.int32, (STRIDE + 2, Q, RING), 0)
    chunk = lax.broadcasted_iota(jnp.int32, (STRIDE + 2, Q, RING), 1)
    lane = lax.broadcasted_iota(jnp.int32, (STRIDE + 2, Q, RING), 2)
    at = chunk * STRIDE + slab
    place = at - 4
    place = jnp.where(place < 0, place + RING, place)
    pmat[...] = jnp.where(place == lane, 1.0, 0.0).reshape(ROWS_X, RING).astype(BF)
    qmat[...] = jnp.where(at == lane, 1.0, 0.0).reshape(ROWS_X, RING)[0:ROWS_M].astype(BF)

    m_slab = lax.broadcasted_iota(jnp.int32, (7, Q, 256), 0)
    m_chunk = lax.broadcasted_iota(jnp.int32, (7, Q, 256), 1)
    m_at = m_chunk * STRIDE + m_slab + col * 256
    for layer in range(3):
        inside = (m_at >= 3 - layer) & (m_at < 512 + 3 - layer)
        masks[layer] = jnp.where(inside, 1.0, 0.0).reshape(7 * Q, 256)

    gin[...] = jnp.zeros_like(gin)
    for b in range(3):
        for ch in range(2):
            for a in range(3):
                w = inw_ref[3 * a + b, ch : ch + 1, :].astype(F32)
                gin[2 * b + ch, a : a + 1, :] = w
                gin[2 * b + ch, 16 + a : 17 + a, :] = w
    for r in range(14):
        start = (20 - r) % 16
        block = jnp.concatenate(
            [gin[g, start : start + 16, :] for g in range(6)] + [jnp.zeros((32, 128), F32)], axis=0
        )
        toe[:, r * 128 : (r + 1) * 128] = block.astype(BF)

    gout[...] = jnp.zeros_like(gout)
    for b in range(3):
        for e in range(2):
            for a in range(3):
                gout[2 * b + e, 10 - a : 11 - a, :] = outw_ref[3 * a + b, e : e + 1, :].astype(F32)
    for p in range(5):
        for h in range(2):
            start = 10 - (2 * p + h)
            block = jnp.concatenate([gout[g, start : start + 8, :] for g in range(6)], axis=0)
            wout[:, p * 256 + h * 128 : p * 256 + (h + 1) * 128] = block.astype(BF)

    for layer in range(2):
        for b in range(3):
            wts[layer, b, 0, 0:128, 128:256] = jnp.zeros((128, 128), BF)
            wts[layer, b, 1, 128:256, 0:128] = jnp.zeros((128, 128), BF)

    for copy in image_copies:
        copy.wait_recv()

    lane8 = lax.broadcasted_iota(jnp.int32, (8, RING), 1)
    sub8 = lax.broadcasted_iota(jnp.int32, (8, RING), 0)
    lanes_ok = (lane8 < 256) | ((lane8 < 320) == (col == 0))
    above_ok = jnp.logical_and(lanes_ok, row > 0)
    below_ok = jnp.logical_and(lanes_ok, row < n_rows - 1)
    tiles = [img[t].astype(F32) for t in range(3)]
    parts = []
    for s in range(3):
        mine, above, below = (t[8 * s : 8 * s + 8] for t in tiles)
        parts.append(jnp.where(lanes_ok, mine, 0.0))
        parts.append(
            jnp.where(sub8 < 4, jnp.where(below_ok, below, 0.0), jnp.where(above_ok, above, 0.0))
        )
    blank = jnp.zeros((96, RING), F32)
    stack = jnp.concatenate(
        [parts[0], parts[1], parts[2], parts[3], blank, parts[0], parts[1], parts[4], parts[5], blank],
        axis=0,
    ).astype(BF)
    cols_in = dot(pmat[...], stack, ((1,), (1,)))

    def row_bias(bias, first_row):
        which = first_row + lax.broadcasted_iota(jnp.int32, (1, 256), 1) // 128
        return jnp.where((which >= 0) & (which < rows_all), bias, OFF)

    def twice(vector):
        return jnp.concatenate([vector, vector], axis=1)

    def finish(total, bias, layer):
        y = jnp.maximum(total + bias, 0.0)
        return jnp.concatenate([y[0 : 7 * Q] * masks[layer], y[7 * Q :]], axis=0)

    def hidden(source, target, layer, count, bias, above):
        @pl.loop(0, count)
        def _(p):
            total = None
            for b in range(3):
                for where in range(2):
                    term = dot(source[p + where, b * Q : b * Q + ROWS_M, :], wts[layer, b, where])
                    total = term if total is None else total + term
            bias_here = row_bias(bias, row * tile_rows + 2 * p - above)
            store_slabs(target, p, finish(total, bias_here, layer + 1))

    table = table_ref[...].astype(F32)
    in_bias = inb_ref[...].reshape(1, 128)
    hidden_bias = hb_ref[...]
    for copy in weight_copies:
        copy.wait()

    for k in range(2):
        here = cols_in[:, 128 * k : 128 * k + 128]
        lhs = (
            here[0:ROWS_M]
            + pltpu.roll(here[Q : Q + ROWS_M], 32, 1)
            + pltpu.roll(here[2 * Q : 2 * Q + ROWS_M], 64, 1)
        ).astype(BF)
        embed = jnp.zeros((1, 128), F32)
        for o in range(table.shape[0]):
            embed = embed + jnp.where(off_ref[k] == o, table[o : o + 1], 0.0)
        bias = twice(in_bias + embed)
        for p in range(7):
            total = dot(lhs, toe[:, p * 256 : (p + 1) * 256])
            bias_here = row_bias(bias, row * tile_rows + 2 * p - 3)
            store_slabs(feat, p, finish(total, bias_here, 0))
        hidden(feat, hid1, 0, 6, twice(hidden_bias[0:1]), 2)
        hidden(hid1, hid2, 1, 5, twice(hidden_bias[1:2]), 1)

        flat = None
        for p in range(5):
            term = dot(wout[:, p * 256 : (p + 1) * 256], hid2[p, 0:ROWS_M, :], ((1,), (1,)))
            flat = term if flat is None else flat + term
        high = flat.astype(BF)
        rest = flat - high.astype(F32)
        mid = rest.astype(BF)
        low = (rest - mid.astype(F32)).astype(BF)
        pieces = dot(jnp.concatenate([high, mid, low], axis=0), qmat[...])
        natural = pieces[0:48] + pieces[48:96] + pieces[96:144]
        if k == 0:
            for copy in prior_copies:
                copy.wait_recv()
            own_prior.wait()
            keep = lanes_ok
            for pp in range(2):
                for e in range(2):
                    pri[pp, e, 0:8, :] = jnp.where(above_ok, pri[pp, e, 0:8, :], 0.0)
                    pri[pp, e, 8:16, :] = jnp.where(keep, pri[pp, e, 8:16, :], 0.0)
                    pri[pp, e, 16:24, :] = jnp.where(below_ok, pri[pp, e, 16:24, :], 0.0)
        flow = []
        for e in range(2):
            z0 = natural[8 * e : 8 * e + 8]
            z1 = pltpu.roll(natural[16 + 8 * e : 24 + 8 * e], RING - 1, 1)
            z2 = pltpu.roll(natural[32 + 8 * e : 40 + 8 * e], RING - 2, 1)
            flow.append(max_shift * jnp.tanh((z0 + z1 + z2)[:, 0:256] + outb_ref[e]))
        row_weight = [jnp.maximum(1.0 - jnp.abs(flow[0] - s), 0.0) for s in range(-2, 3)]
        col_weight = [jnp.maximum(1.0 - jnp.abs(flow[1] - s), 0.0) for s in range(-2, 3)]
        mine = pair * 2 + k
        for e in range(2):
            value = flow[e]
            for rs in range(-2, 3):
                band = pri[k, e, 8 + rs : 16 + rs, :]
                inner = None
                for cs in range(-2, 3):
                    moved = band if cs == 0 else pltpu.roll(band, (RING - cs) % RING, 1)
                    term = col_weight[cs + 2] * moved[:, 0:256]
                    inner = term if inner is None else inner + term
                value = value + row_weight[rs + 2] * inner
            cand_ref[k, e] = value
            every[mine, e] = value
        copy = pltpu.make_async_remote_copy(
            src_ref=every.at[mine],
            dst_ref=every.at[mine],
            send_sem=cand_send.at[k],
            recv_sem=cand_recv.at[k],
            device_id=(partner, row, col),
            device_id_type=MESH,
        )
        copy.start()
        if k == 0:
            first_copy = copy
        else:
            second_copy = copy

    first_copy.wait()
    second_copy.wait()
    c = [[every[k, e] for e in range(2)] for k in range(4)]
    score = [None] * 4
    for i in range(4):
        for j in range(i + 1, 4):
            dr = c[i][0] - c[j][0]
            dc = c[i][1] - c[j][1]
            apart = dr * dr + dc * dc
            score[i] = apart if score[i] is None else score[i] + apart
            score[j] = apart if score[j] is None else score[j] + apart
    weight = [jnp.exp(score[i] * (-1.0 / (3 * sharpness))) for i in range(4)]
    bottom = (weight[0] + weight[1]) + (weight[2] + weight[3])
    for e in range(2):
        top = (weight[0] * c[0][e] + weight[1] * c[1][e]) + (
            weight[2] * c[2][e] + weight[3] * c[3][e]
        )
        vote_ref[e] = top / bottom

    for copy in image_copies + prior_copies:
        copy.wait_send()


def solution(mesh):
    n_rows = mesh.shape["rows"]
    in_specs = (
        P("rows", "cols"),
        P("pair", "rows", "cols"),
        P("pair", None, "rows", "cols"),
        P("pair"),
        P(),
        P(),
        P(),
        P(),
        P(),
        P(),
        P(),
    )
    out_specs = (P("pair", None, "rows", "cols"), P(None, "rows", "cols"))
    vmem = pl.BlockSpec(memory_space=pltpu.VMEM)
    smem = pl.BlockSpec(memory_space=pltpu.SMEM)
    anywhere = pl.BlockSpec(memory_space=pl.ANY)
    dma = pltpu.SemaphoreType.DMA

    def shards(*args):
        return pl.pallas_call(
            functools.partial(kernel, n_rows),
            out_shape=(
                jax.ShapeDtypeStruct((2, 2, 8, 256), F32),
                jax.ShapeDtypeStruct((2, 8, 256), F32),
            ),
            in_specs=[vmem, vmem, anywhere, smem, vmem, vmem, vmem, anywhere, vmem, vmem, smem],
            out_specs=(vmem, vmem),
            scratch_shapes=[
                pltpu.VMEM((3, 32, RING), BF),
                pltpu.VMEM((32, 128), BF),
                pltpu.VMEM((2, 2, 24, RING), F32),
                pltpu.VMEM((2, 3, 2, 256, 256), BF),
                pltpu.VMEM((ROWS_X, RING), BF),
                pltpu.VMEM((ROWS_M, RING), BF),
                pltpu.VMEM((6, 32, 128), F32),
                pltpu.VMEM((128, 14 * 128), BF),
                pltpu.VMEM((6, 24, 128), F32),
                pltpu.VMEM((48, 5 * 256), BF),
                pltpu.VMEM((7, ROWS_X, 256), BF),
                pltpu.VMEM((6, ROWS_X, 256), BF),
                pltpu.VMEM((5, ROWS_X, 256), BF),
                pltpu.VMEM((3, 7 * Q, 256), F32),
                pltpu.VMEM((4, 2, 8, 256), F32),
                dma((6,)),
                dma,
                dma((5,)),
                dma((5,)),
                dma((5,)),
                dma((5,)),
                dma((2,)),
                dma((2,)),
            ],
            compiler_params=pltpu.CompilerParams(
                collective_id=0, has_side_effects=True, vmem_limit_bytes=32 * 1024 * 1024
            ),
        )(*args)

    return jax.shard_map(shards, mesh=mesh, in_specs=in_specs, out_specs=out_specs, check_vma=False)
```

time: 119 us -> 39.8 us (0.33)
  the two profiles are of different devices: /device:TPU:126 before, /device:TPU:1 now
where the time goes in v1:
time: 39.8 us; the launch traced here: 39.4 us
  Pallas kernels  29.6 us (74%)
  local copies, waits for them, and re-layouts  9.12 us (23%)
  between operations  0.66 us (2%)
    pallas_call x1, Pallas kernels, shards(): pl.pallas_call(functools.partial(kernel, n_rows), out_shape=(jax.ShapeDty...  29.6 us
    unnamed x24, local copies, waits for them, and re-layouts  9.12 us

profile of v1, /device:TPU:1, one launch (start us, length us, event | category | flops | bytes accessed | tf_op | source)
XLA Modules:
  0.0 39.4 jit_solution(4094457266117945747)
XLA Ops:
  0.6 0.0 copy-start
  0.6 1.1 %copy-done = bf16[2,9,128,128]{3,2,1,0:T(8,128)(2,1)S(1)} copy-done((bf16[2,9,128,128]{3,2,1,0:T(8,128)(2,1)S(1)}, bf16[2,9,128,128]{3,2,1,0:T(8,128)(2,1)}, u32[]{:S(2)}) %copy-start) | copy-done | bytes 589848
  1.7 0.0 copy-start.1
  1.7 0.8 %copy-done.1 = f32[2,2,8,256]{3,2,1,0:T(8,128)S(1)} copy-done((f32[2,2,8,256]{3,2,1,0:T(8,128)S(1)}, f32[2,2,8,256]{3,2,1,0:T(8,128)}, u32[]{:S(2)}) %copy-start.1) | copy-done | bytes 32792
  2.5 0.0 copy-start.2
  2.5 0.7 %copy-done.2 = bf16[2,8,256]{2,1,0:T(8,128)(2,1)S(1)} copy-done((bf16[2,8,256]{2,1,0:T(8,128)(2,1)S(1)}, bf16[2,8,256]{2,1,0:T(8,128)(2,1)}, u32[]{:S(2)}) %copy-start.2) | copy-done | bytes 8216
  3.2 0.0 copy-start.3
  3.2 0.7 %copy-done.3 = bf16[9,2,128]{2,1,0:T(2,128)(2,1)S(1)} copy-done((bf16[9,2,128]{2,1,0:T(2,128)(2,1)S(1)}, bf16[9,2,128]{2,1,0:T(2,128)(2,1)}, u32[]{:S(2)}) %copy-start.3) | copy-done | bytes 4632
  3.8 0.0 copy-start.4
  3.8 0.7 %copy-done.4 = bf16[9,2,128]{2,1,0:T(2,128)(2,1)S(1)} copy-done((bf16[9,2,128]{2,1,0:T(2,128)(2,1)S(1)}, bf16[9,2,128]{2,1,0:T(2,128)(2,1)}, u32[]{:S(2)}) %copy-start.4) | copy-done | bytes 4632
  4.5 0.0 copy-start.5
  4.5 0.7 %copy-done.5 = bf16[8,256]{1,0:T(8,128)(2,1)S(1)} copy-done((bf16[8,256]{1,0:T(8,128)(2,1)S(1)}, bf16[8,256]{1,0:T(8,128)(2,1)}, u32[]{:S(2)}) %copy-start.5) | copy-done | bytes 4120
  5.2 0.0 copy-start.6
  5.2 0.7 %copy-done.6 = bf16[3,128]{1,0:T(4,128)(2,1)S(1)} copy-done((bf16[3,128]{1,0:T(4,128)(2,1)S(1)}, bf16[3,128]{1,0:T(4,128)(2,1)}, u32[]{:S(2)}) %copy-start.6) | copy-done | bytes 792
  5.9 0.0 copy-start.7
  5.9 0.7 %copy-done.7 = f32[2,128]{1,0:T(2,128)S(1)} copy-done((f32[2,128]{1,0:T(2,128)S(1)}, f32[2,128]{1,0:T(2,128)}, u32[]{:S(2)}) %copy-start.7) | copy-done | bytes 1048
  6.6 0.0 copy-start.8
  6.6 0.7 %copy-done.8 = s32[2]{0:T(128)S(1)} copy-done((s32[2]{0:T(128)S(1)}, s32[2]{0:T(128)}, u32[]{:S(2)}) %copy-start.8) | copy-done | bytes 32
  7.2 0.0 copy-start.9
  7.2 0.7 %copy-done.9 = f32[128]{0:T(128)S(1)} copy-done((f32[128]{0:T(128)S(1)}, f32[128]{0:T(128)}, u32[]{:S(2)}) %copy-start.9) | copy-done | bytes 536
  7.9 0.0 copy-start.10
  7.9 0.7 %copy-done.10 = f32[2]{0:T(128)S(1)} copy-done((f32[2]{0:T(128)S(1)}, f32[2]{0:T(128)}, u32[]{:S(2)}) %copy-start.10) | copy-done | bytes 32
  8.5 29.6 %shard_map.122 = (f32[2,2,8,256]{3,2,1,0:T(8,128)S(1)}, f32[2,8,256]{2,1,0:T(8,128)S(1)}) custom-call(bf16[8,256]{1,0:T(8,128)(2,1)S(1)} %copy-done.5, bf16[2,8,256]{2,1,0:T(8,128)(2,1)S(1)} %copy-done.2, f32[2,2,8,256]{3,2,1,0:T(8,128)S(1)} %copy-done.1, s32[2]{0:T(128)S(1)} %copy-done.8, bf16[3,128]{1,0:T(4,128)(2,1)S(1)} %copy-done.6, ...), custom_call_target="tpu_custom_call" | custom-call | tf_op jit(solution)/shard_map/pallas_call | solution.py:365
  38.2 0.6 %copy.15 = f32[2,2,8,256]{3,2,1,0:T(8,128)} copy(f32[2,2,8,256]{3,2,1,0:T(8,128)S(1)} %get-tuple-element.4) | data formatting | bytes 65536
  38.8 0.6 %copy.16 = f32[2,8,256]{2,1,0:T(8,128)} copy(f32[2,8,256]{2,1,0:T(8,128)S(1)} %get-tuple-element.5) | data formatting | bytes 32768
Async XLA Ops:
  0.6 1.1 %copy-start = (bf16[2,9,128,128]{3,2,1,0:T(8,128)(2,1)S(1)}, bf16[2,9,128,128]{3,2,1,0:T(8,128)(2,1)}, u32[]{:S(2)}) copy-start(bf16[2,9,128,128]{3,2,1,0:T(8,128)(2,1)} %hw_ref.1) | copy-start | bytes 1769476
  1.7 0.8 %copy-start.1 = (f32[2,2,8,256]{3,2,1,0:T(8,128)S(1)}, f32[2,2,8,256]{3,2,1,0:T(8,128)}, u32[]{:S(2)}) copy-start(f32[2,2,8,256]{3,2,1,0:T(8,128)} %prior_ref.1) | copy-start | bytes 98308
  2.5 0.7 %copy-start.2 = (bf16[2,8,256]{2,1,0:T(8,128)(2,1)S(1)}, bf16[2,8,256]{2,1,0:T(8,128)(2,1)}, u32[]{:S(2)}) copy-start(bf16[2,8,256]{2,1,0:T(8,128)(2,1)} %tgt_ref.1) | copy-start | bytes 24580
  3.2 0.7 %copy-start.3 = (bf16[9,2,128]{2,1,0:T(2,128)(2,1)S(1)}, bf16[9,2,128]{2,1,0:T(2,128)(2,1)}, u32[]{:S(2)}) copy-start(bf16[9,2,128]{2,1,0:T(2,128)(2,1)} %inw_ref.1) | copy-start | bytes 13828
  3.8 0.7 %copy-start.4 = (bf16[9,2,128]{2,1,0:T(2,128)(2,1)S(1)}, bf16[9,2,128]{2,1,0:T(2,128)(2,1)}, u32[]{:S(2)}) copy-start(bf16[9,2,128]{2,1,0:T(2,128)(2,1)} %outw_ref.1) | copy-start | bytes 13828
  4.5 0.7 %copy-start.5 = (bf16[8,256]{1,0:T(8,128)(2,1)S(1)}, bf16[8,256]{1,0:T(8,128)(2,1)}, u32[]{:S(2)}) copy-start(bf16[8,256]{1,0:T(8,128)(2,1)} %src_ref.1) | copy-start | bytes 12292
  5.2 0.7 %copy-start.6 = (bf16[3,128]{1,0:T(4,128)(2,1)S(1)}, bf16[3,128]{1,0:T(4,128)(2,1)}, u32[]{:S(2)}) copy-start(bf16[3,128]{1,0:T(4,128)(2,1)} %table_ref.1) | copy-start | bytes 2308
  5.9 0.7 %copy-start.7 = (f32[2,128]{1,0:T(2,128)S(1)}, f32[2,128]{1,0:T(2,128)}, u32[]{:S(2)}) copy-start(f32[2,128]{1,0:T(2,128)} %hb_ref.1) | copy-start | bytes 3076
  6.6 0.7 %copy-start.8 = (s32[2]{0:T(128)S(1)}, s32[2]{0:T(128)}, u32[]{:S(2)}) copy-start(s32[2]{0:T(128)} %off_ref.1) | copy-start | bytes 28
  7.2 0.7 %copy-start.9 = (f32[128]{0:T(128)S(1)}, f32[128]{0:T(128)}, u32[]{:S(2)}) copy-start(f32[128]{0:T(128)} %inb_ref.1) | copy-start | bytes 1540
  7.9 0.7 %copy-start.10 = (f32[2]{0:T(128)S(1)}, f32[2]{0:T(128)}, u32[]{:S(2)}) copy-start(f32[2]{0:T(128)} %outb_ref.1) | copy-start | bytes 28

commit v2 on v1

--- a/solution.py
+++ b/solution.py
@@ -35,19 +35,27 @@
 
 def kernel(
     n_rows,
+    src_in,
+    tgt_in,
+    prior_ref,
+    off_in,
+    table_in,
+    inw_in,
+    inb_in,
+    hw_ref,
+    hb_in,
+    outw_in,
+    outb_in,
+    every,
     src_ref,
     tgt_ref,
-    prior_ref,
     off_ref,
     table_ref,
     inw_ref,
     inb_ref,
-    hw_ref,
     hb_ref,
     outw_ref,
     outb_ref,
-    cand_ref,
-    vote_ref,
     img,
     side,
     pri,
@@ -62,7 +70,7 @@
     hid1,
     hid2,
     masks,
-    every,
+    in_sem,
     w_sem,
     p_sem,
     img_send,
@@ -93,6 +101,24 @@
     for place in places + ((partner, row, col),):
         pl.semaphore_signal(barrier, inc=1, device_id=place, device_id_type=MESH)
 
+    loads = []
+    for number, (source, target) in enumerate(
+        (
+            (src_in, src_ref),
+            (tgt_in, tgt_ref),
+            (inw_in, inw_ref),
+            (outw_in, outw_ref),
+            (off_in, off_ref),
+            (table_in, table_ref),
+            (inb_in, inb_ref),
+            (hb_in, hb_ref),
+            (outb_in, outb_ref),
+        )
+    ):
+        copy = pltpu.make_async_copy(source, target, in_sem.at[number])
+        copy.start()
+        loads.append(copy)
+
     weight_copies = []
     for number, (a, where, r0, l0) in enumerate(
         ((0, 0, 0, 0), (1, 0, 128, 0), (0, 0, 128, 128), (2, 1, 0, 0), (1, 1, 0, 128), (2, 1, 128, 128))
@@ -109,6 +135,8 @@
     )
     own_prior.start()
 
+    for copy in loads[:2]:
+        copy.wait()
     src = src_ref[...].astype(F32)
     tgt = tgt_ref[...].astype(F32)
     own = jnp.concatenate([src, tgt[0], tgt[1], jnp.zeros_like(src)], axis=0).astype(BF)
@@ -163,6 +191,8 @@
         inside = (m_at >= 3 - layer) & (m_at < 512 + 3 - layer)
         masks[layer] = jnp.where(inside, 1.0, 0.0).reshape(7 * Q, 256)
 
+    for copy in loads[2:]:
+        copy.wait()
     gin[...] = jnp.zeros_like(gin)
     for b in range(3):
         for ch in range(2):
@@ -228,7 +258,7 @@
         return jnp.concatenate([y[0 : 7 * Q] * masks[layer], y[7 * Q :]], axis=0)
 
     def hidden(source, target, layer, count, bias, above):
-        @pl.loop(0, count)
+        @pl.loop(0, count, unroll=count)
         def _(p):
             total = None
             for b in range(3):
@@ -301,7 +331,6 @@
                     term = col_weight[cs + 2] * moved[:, 0:256]
                     inner = term if inner is None else inner + term
                 value = value + row_weight[rs + 2] * inner
-            cand_ref[k, e] = value
             every[mine, e] = value
         copy = pltpu.make_async_remote_copy(
             src_ref=every.at[mine],
@@ -319,6 +348,14 @@
 
     first_copy.wait()
     second_copy.wait()
+    for copy in image_copies + prior_copies:
+        copy.wait_send()
+
+
+def vote(every, cand_ref, vote_ref):
+    pair = lax.axis_index("pair")
+    for k in range(2):
+        cand_ref[k] = every[2 * pair + k]
     c = [[every[k, e] for e in range(2)] for k in range(4)]
     score = [None] * 4
     for i in range(4):
@@ -336,9 +373,6 @@
         )
         vote_ref[e] = top / bottom
 
-    for copy in image_copies + prior_copies:
-        copy.wait_send()
-
 
 def solution(mesh):
     n_rows = mesh.shape["rows"]
@@ -357,20 +391,26 @@
     )
     out_specs = (P("pair", None, "rows", "cols"), P(None, "rows", "cols"))
     vmem = pl.BlockSpec(memory_space=pltpu.VMEM)
-    smem = pl.BlockSpec(memory_space=pltpu.SMEM)
-    anywhere = pl.BlockSpec(memory_space=pl.ANY)
+    hbm = pl.BlockSpec(memory_space=pltpu.HBM)
     dma = pltpu.SemaphoreType.DMA
 
     def shards(*args):
-        return pl.pallas_call(
+        args = [pltpu.with_memory_space_constraint(x, pltpu.HBM) for x in args]
+        every = pl.pallas_call(
             functools.partial(kernel, n_rows),
-            out_shape=(
-                jax.ShapeDtypeStruct((2, 2, 8, 256), F32),
-                jax.ShapeDtypeStruct((2, 8, 256), F32),
-            ),
-            in_specs=[vmem, vmem, anywhere, smem, vmem, vmem, vmem, anywhere, vmem, vmem, smem],
-            out_specs=(vmem, vmem),
+            out_shape=pltpu.VMEM((4, 2, 8, 256), F32),
+            in_specs=[hbm] * 11,
+            out_specs=vmem,
             scratch_shapes=[
+                pltpu.VMEM((8, 256), BF),
+                pltpu.VMEM((2, 8, 256), BF),
+                pltpu.SMEM((2,), jnp.int32),
+                pltpu.VMEM((3, 128), BF),
+                pltpu.VMEM((9, 2, 128), BF),
+                pltpu.VMEM((128,), F32),
+                pltpu.VMEM((2, 128), F32),
+                pltpu.VMEM((9, 2, 128), BF),
+                pltpu.SMEM((2,), F32),
                 pltpu.VMEM((3, 32, RING), BF),
                 pltpu.VMEM((32, 128), BF),
                 pltpu.VMEM((2, 2, 24, RING), F32),
@@ -385,7 +425,7 @@
                 pltpu.VMEM((6, ROWS_X, 256), BF),
                 pltpu.VMEM((5, ROWS_X, 256), BF),
                 pltpu.VMEM((3, 7 * Q, 256), F32),
-                pltpu.VMEM((4, 2, 8, 256), F32),
+                dma((9,)),
                 dma((6,)),
                 dma,
                 dma((5,)),
@@ -396,8 +436,17 @@
                 dma((2,)),
             ],
             compiler_params=pltpu.CompilerParams(
-                collective_id=0, has_side_effects=True, vmem_limit_bytes=32 * 1024 * 1024
+                collective_id=0, has_side_effects=True, vmem_limit_bytes=40 * 1024 * 1024
             ),
         )(*args)
+        return pl.pallas_call(
+            vote,
+            out_shape=(
+                jax.ShapeDtypeStruct((2, 2, 8, 256), F32),
+                jax.ShapeDtypeStruct((2, 8, 256), F32),
+            ),
+            in_specs=[vmem],
+            out_specs=(vmem, vmem),
+        )(pltpu.with_memory_space_constraint(every, pltpu.VMEM))
 
     return jax.shard_map(shards, mesh=mesh, in_specs=in_specs, out_specs=out_specs, check_vma=False)

time: 39.8 us -> 26.3 us (0.66)
  local copies, waits for them, and re-layouts: 9.12 us -> 0 us
  Pallas kernels: 29.6 us -> 25.6 us
    unnamed x24 -> x0, local copies, waits for them, and re-layouts: 9.12 us -> none
    pallas_call x1 -> x2, Pallas kernels: 29.6 us -> 25.6 us  [the longest x1 24.9 us: shards(): pl.pallas_call(functools.partial(kernel, n_rows), out_shape=pltpu.VMEM((4...]
where the time goes in v2:
time: 26.3 us; the launch traced here: 26.2 us
  Pallas kernels  25.6 us (97%)
  between operations  0.64 us (2%)
    pallas_call x1, Pallas kernels, shards(): pl.pallas_call(functools.partial(kernel, n_rows), out_shape=pltpu.VMEM((4...  24.9 us
    pallas_call x1, Pallas kernels, shards(): pl.pallas_call(vote, out_shape=(jax.ShapeDtypeStruct((2, 2, 8, 256), F32)...  0.64 us

profile of v2, /device:TPU:1, one launch (start us, length us, event | category | flops | bytes accessed | tf_op | source)
XLA Modules:
  0.0 26.2 jit_solution(3169535379787328937)
XLA Ops:
  0.6 24.9 %shard_map.122.every = f32[4,2,8,256]{3,2,1,0:T(8,128)S(1)} custom-call(bf16[8,256]{1,0:T(8,128)(2,1)} %src_in.1, bf16[2,8,256]{2,1,0:T(8,128)(2,1)} %tgt_in.1, f32[2,2,8,256]{3,2,1,0:T(8,128)} %prior_ref.1, s32[2]{0:T(128)} %off_in.1, bf16[3,128]{1,0:T(4,128)(2,1)} %table_in.1, bf16[9,2,128]{2,1,0:T(2,128)(2,1)} %inw_in.1, f32[128]{0:T(128)} %inb_in.1, ...), custom_call_target="tpu_custom_call" | custom-call | tf_op jit(solution)/shard_map/pallas_call | solution.py:399
  25.6 0.6 %shard_map.123 = (f32[2,2,8,256]{3,2,1,0:T(8,128)}, f32[2,8,256]{2,1,0:T(8,128)}) custom-call(f32[4,2,8,256]{3,2,1,0:T(8,128)S(1)} %shard_map.122.every), custom_call_target="tpu_custom_call" | custom-call | tf_op jit(solution)/shard_map/pallas_call | solution.py:442

commit v3 on v2

v3 whole, which is shorter than its diff:
```python
import functools

import jax
import jax.numpy as jnp
from jax import lax
from jax.experimental import pallas as pl
from jax.experimental.pallas import tpu as pltpu
from jax.sharding import PartitionSpec as P

MESH = pl.DeviceIdType.MESH
BF = jnp.bfloat16
F32 = jnp.float32

sharpness = 4.0
max_shift = 2.0
OFF = -1e30

Q = 16
STRIDE = 17
ROWS_M = STRIDE * Q
ROWS_X = (STRIDE + 2) * Q
RING = 384


def dot(a, b, dims=((1,), (0,))):
    return lax.dot_general(a, b, (dims, ((), ())), preferred_element_type=F32)


def store_slabs(ref, index, y):
    ref[index, 0:ROWS_M, :] = y.astype(BF)
    first = pltpu.roll(y[0:Q], Q - 1, 0)
    second = pltpu.roll(y[Q : 2 * Q], Q - 1, 0)
    ref[index, ROWS_M:ROWS_X, :] = jnp.concatenate([first, second], axis=0).astype(BF)


def kernel(
    n_rows,
    src_in,
    tgt_in,
    prior_ref,
    off_in,
    table_in,
    inw_in,
    inb_in,
    hw_ref,
    hb_in,
    outw_in,
    outb_in,
    every,
    off_ref,
    table_ref,
    inw_ref,
    inb_ref,
    hb_ref,
    outw_ref,
    outb_ref,
    img,
    side,
    own_s,
    own_t,
    pri,
    wts,
    turned,
    order,
    gin,
    toe,
    gout,
    wout,
    feat,
    hid1,
    part1,
    part2,
    sums_out,
    part_of,
    bands,
    masks,
    in_sem,
    w_sem,
    p_sem,
    img_send,
    img_recv,
    pri_send,
    pri_recv,
    cand_send,
    cand_recv,
):
    pair = lax.axis_index("pair")
    row = lax.axis_index("rows")
    col = lax.axis_index("cols")
    has_up = row > 0
    has_down = row < n_rows - 1
    up = jnp.maximum(row - 1, 0)
    down = jnp.minimum(row + 1, n_rows - 1)
    other = 1 - col
    partner = 1 - pair
    tile_rows = 8
    rows_all = n_rows * tile_rows
    places = (
        (pair, up, col),
        (pair, down, col),
        (pair, row, other),
        (pair, up, other),
        (pair, down, other),
    )

    sends_to = (has_up, has_down, None, has_up, has_down)
    comes_from = (has_down, has_up, None, has_down, has_up)

    def only_if(condition, action):
        if condition is None:
            action()
        else:
            pl.when(condition)(action)

    def signal(place):
        pl.semaphore_signal(barrier, inc=1, device_id=place, device_id_type=MESH)

    barrier = pltpu.get_barrier_semaphore()
    for number in (0, 3, 1, 4, 2):
        only_if(sends_to[number], functools.partial(signal, places[number]))
    signal((partner, row, col))

    loads = []
    for number, (source, target) in enumerate(
        (
            (src_in, own_s),
            (tgt_in, own_t),
            (inw_in, inw_ref),
            (outw_in, outw_ref),
            (off_in, off_ref),
            (table_in, table_ref),
            (inb_in, inb_ref),
            (hb_in, hb_ref),
            (outb_in, outb_ref),
        )
    ):
        copy = pltpu.make_async_copy(source, target, in_sem.at[number])
        copy.start()
        loads.append(copy)

    weight_copies = []
    for number, (a, where, r0, l0) in enumerate(
        ((0, 0, 0, 0), (1, 0, 128, 0), (0, 0, 128, 128), (2, 1, 0, 0), (1, 1, 0, 128), (2, 1, 128, 128))
    ):
        copy = pltpu.make_async_copy(
            hw_ref.at[:, pl.ds(3 * a, 3)],
            wts.at[:, :, where, pl.ds(r0, 128), pl.ds(l0, 128)],
            w_sem.at[number],
        )
        copy.start()
        weight_copies.append(copy)
    own_prior = pltpu.make_async_copy(
        prior_ref, pri.at[:, :, pl.ds(8, 8), pl.ds(0, 256)], p_sem
    )
    own_prior.start()

    for copy in loads[:2]:
        copy.wait()
    own_rows = [own_s[...], own_t[0], own_t[1]]
    own = jnp.concatenate(
        [x.astype(F32) for x in own_rows] + [jnp.zeros((8, 256), F32)], axis=0
    ).astype(BF)
    img[0, :, 0:256] = own
    side[...] = jnp.where(col == 0, own[:, 128:256], own[:, 0:128])
    order[...] = jnp.zeros_like(order)

    m_slab = lax.broadcasted_iota(jnp.int32, (7, Q, 256), 0)
    m_chunk = lax.broadcasted_iota(jnp.int32, (7, Q, 256), 1)
    m_at = m_chunk * STRIDE + m_slab + col * 256
    for layer in range(3):
        inside = (m_at >= 3 - layer) & (m_at < 512 + 3 - layer)
        masks[layer] = jnp.where(inside, 1.0, 0.0).reshape(7 * Q, 256)

    for copy in loads[2:]:
        copy.wait()
    gin[...] = jnp.zeros_like(gin)
    for b in range(3):
        for ch in range(2):
            for a in range(3):
                w = inw_ref[3 * a + b, ch : ch + 1, :].astype(F32)
                gin[2 * b + ch, a : a + 1, :] = w
                gin[2 * b + ch, 16 + a : 17 + a, :] = w
    for r in range(14):
        start = (20 - r) % 16
        block = jnp.concatenate(
            [gin[g, start : start + 16, :] for g in range(6)] + [jnp.zeros((32, 128), F32)], axis=0
        )
        toe[:, r * 128 : (r + 1) * 128] = block.astype(BF)

    gout[...] = jnp.zeros_like(gout)
    for b in range(3):
        for e in range(2):
            for a in range(3):
                gout[2 * b + e, 10 - a : 11 - a, :] = outw_ref[3 * a + b, e : e + 1, :].astype(F32)
    for p in range(5):
        for h in range(2):
            start = 10 - (2 * p + h)
            block = jnp.concatenate(
                [gout[g, start : start + 8, :] for g in range(6)] + [jnp.zeros((80, 128), F32)], axis=0
            )
            wout[p, h * 128 : (h + 1) * 128, :] = jnp.transpose(block).astype(BF)

    for layer in range(2):
        for b in range(3):
            wts[layer, b, 0, 0:128, 128:256] = jnp.zeros((128, 128), BF)
            wts[layer, b, 1, 128:256, 0:128] = jnp.zeros((128, 128), BF)

    pl.semaphore_wait(barrier, 2 + 2 * has_up.astype(jnp.int32) + 2 * has_down.astype(jnp.int32))

    main = pl.ds(0, 256)
    edge = pl.ds(256, 128)
    half = pl.ds(pl.multiple_of((1 - col) * 128, 128), 128)
    routes = ((2, main), (1, main), (0, edge), (2, edge), (1, edge))
    image_copies = [None] * 5
    for number in (0, 3, 1, 4, 2):
        slot, lanes = routes[number]
        copy = pltpu.make_async_remote_copy(
            src_ref=img.at[0, :, main] if number < 2 else side,
            dst_ref=img.at[slot, :, lanes],
            send_sem=img_send.at[number],
            recv_sem=img_recv.at[number],
            device_id=places[number],
            device_id_type=MESH,
        )
        only_if(sends_to[number], copy.start)
        image_copies[number] = copy
    prior_copies = []
    for number, (slot, lanes) in enumerate(routes):
        start = (8, 0, 16)[slot]
        copy = pltpu.make_async_remote_copy(
            src_ref=prior_ref if number < 2 else prior_ref.at[:, :, :, half],
            dst_ref=pri.at[:, :, pl.ds(start, 8), lanes],
            send_sem=pri_send.at[number],
            recv_sem=pri_recv.at[number],
            device_id=places[number],
            device_id_type=MESH,
        )
        only_if(sends_to[number], copy.start)
        prior_copies.append(copy)

    lane8 = lax.broadcasted_iota(jnp.int32, (8, RING), 1)
    sub8 = lax.broadcasted_iota(jnp.int32, (8, RING), 0)
    lanes_ok = (lane8 < 256) | ((lane8 < 320) == (col == 0))
    above_ok = jnp.logical_and(lanes_ok, has_up)
    below_ok = jnp.logical_and(lanes_ok, has_down)
    blank = jnp.zeros((8, RING), F32)

    def gather_columns(rows_of):
        three = [rows_of(s) for s in range(3)]
        space = [blank] * 4
        stack = jnp.concatenate(
            list(three[0] + three[1]) + space + list(three[0] + three[2]) + space, axis=0
        )
        turned[4 : RING + 4, :] = jnp.transpose(stack)
        turned[0:4, :] = turned[RING : RING + 4, :]
        slabs = [turned[pl.ds(i, Q, STRIDE), :] for i in range(STRIDE + 2)]
        group = lax.broadcasted_iota(jnp.int32, (ROWS_M, 128), 1) // 32
        out = []
        for k in range(2):
            moved = [
                jnp.concatenate(slabs[b : b + STRIDE], axis=0)
                if (32 * b - 64 * k) % 128 == 0
                else pltpu.roll(jnp.concatenate(slabs[b : b + STRIDE], axis=0), (32 * b - 64 * k) % 128, 1)
                for b in range(3)
            ]
            out.append(
                jnp.where(group == 0, moved[0], jnp.where(group == 1, moved[1], moved[2])).astype(BF)
            )
        return out

    def image(slot, s):
        return img[slot].astype(F32)[8 * s : 8 * s + 8]

    def own_image(s):
        return (jnp.where(lanes_ok, image(0, s), 0.0), blank)

    def halo_rows(s):
        above = jnp.where(above_ok, image(1, s), 0.0)
        below = jnp.where(below_ok, image(2, s), 0.0)
        return (blank, jnp.where(sub8 < 4, below, above))

    def row_bias(bias, first_row):
        which = first_row + lax.broadcasted_iota(jnp.int32, (1, 256), 1) // 128
        return jnp.where((which >= 0) & (which < rows_all), bias, OFF)

    def twice(vector):
        return jnp.concatenate([vector, vector], axis=1)

    def finish(total, bias, layer):
        y = jnp.maximum(total + bias, 0.0)
        return jnp.concatenate([y[0 : 7 * Q] * masks[layer], y[7 * Q :]], axis=0)

    def first_layer(k, p, lhs):
        total = dot(lhs, toe[:, p * 256 : (p + 1) * 256])
        bias_here = row_bias(first_bias[k], row * tile_rows + 2 * p - 3)
        store_slabs(feat.at[k], p, finish(total, bias_here, 0))

    def taps(source, k, p, layer, wheres):
        total = None
        for where in wheres:
            for b in range(3):
                term = dot(source[k, p + where, b * Q : b * Q + ROWS_M, :], wts[layer, b, where])
                total = term if total is None else total + term
        return total

    hidden_layers = ((feat, part1), (hid1, part2))

    def hidden(k, p, layer, wheres=(0, 1), part=None):
        source, sums = hidden_layers[layer]
        total = taps(source, k, p, layer, wheres)
        if part is not None:
            total = total + sums[k, part]
        bias_here = row_bias(hidden_bias[layer], row * tile_rows + 2 * p - 2 + layer)
        y = finish(total, bias_here, layer + 1)
        if layer == 0:
            store_slabs(hid1.at[k], p, y)
            return None
        part_of[k, p] = y.astype(BF)
        return None

    def partial(k, p, layer, where, part):
        source, sums = hidden_layers[layer]
        sums[k, part] = taps(source, k, p, layer, (where,))

    table = table_ref[...].astype(F32)
    in_bias = inb_ref[...].reshape(1, 128)
    hidden_bias = [twice(hb_ref[layer : layer + 1, :]) for layer in range(2)]
    first_bias = []
    for k in range(2):
        embed = jnp.zeros((1, 128), F32)
        for o in range(table.shape[0]):
            embed = embed + jnp.where(off_ref[k] == o, table[o : o + 1], 0.0)
        first_bias.append(twice(in_bias + embed))

    image_copies[2].wait_recv()
    lhs_own = gather_columns(own_image)
    for k in range(2):
        for p in (2, 3, 4):
            first_layer(k, p, lhs_own[k])
    for copy in weight_copies:
        copy.wait()
    for k in range(2):
        for p in (2, 3):
            hidden(k, p, 0)
    for k in range(2):
        partial(k, 1, 0, 1, 0)
        partial(k, 4, 0, 0, 1)
    for k in range(2):
        hidden(k, 2, 1)
    for k in range(2):
        partial(k, 1, 1, 1, 0)
        partial(k, 3, 1, 0, 1)
    for k in range(2):
        sums_out[k] = dot(part_of[k, 2], wout[2])

    for number in (0, 1, 3, 4):
        only_if(comes_from[number], image_copies[number].wait_recv)
    lhs = [a + b for a, b in zip(lhs_own, gather_columns(halo_rows))]
    for k in range(2):
        for p in (0, 1, 5, 6):
            first_layer(k, p, lhs[k])
    for k in range(2):
        hidden(k, 0, 0)
        hidden(k, 1, 0, (0,), 0)
        hidden(k, 4, 0, (1,), 1)
        hidden(k, 5, 0)
    for number in range(5):
        only_if(comes_from[number], prior_copies[number].wait_recv)
    own_prior.wait()
    for k in range(2):
        hidden(k, 0, 1)
        hidden(k, 1, 1, (0,), 0)
        hidden(k, 3, 1, (1,), 1)
        hidden(k, 4, 1)
    flat = []
    for k in range(2):
        total = sums_out[k]
        for p in (0, 1, 3, 4):
            total = total + dot(part_of[k, p], wout[p])
        flat.append(total)
    for k in range(2):
        for e in range(2):
            pri[k, e, 0:8, :] = jnp.where(above_ok, pri[k, e, 0:8, :], 0.0)
            pri[k, e, 8:16, :] = jnp.where(lanes_ok, pri[k, e, 8:16, :], 0.0)
            pri[k, e, 16:24, :] = jnp.where(below_ok, pri[k, e, 16:24, :], 0.0)
            for rs in range(5):
                band = pri[k, e, 6 + rs : 14 + rs, :]
                for cs in range(5):
                    moved = band if cs == 2 else pltpu.roll(band, (RING + 2 - cs) % RING, 1)
                    bands[k, e, rs, cs] = moved[:, 0:256]

    for k in range(2):
        for i in range(STRIDE):
            order[k, pl.ds(i, Q, STRIDE), :] = flat[k][i * Q : (i + 1) * Q]
        natural = jnp.transpose(order[k])
        flow = []
        for e in range(2):
            z0 = natural[8 * e : 8 * e + 8]
            z1 = pltpu.roll(natural[16 + 8 * e : 24 + 8 * e], RING - 1, 1)
            z2 = pltpu.roll(natural[32 + 8 * e : 40 + 8 * e], RING - 2, 1)
            flow.append(max_shift * jnp.tanh((z0 + z1 + z2)[:, 0:256] + outb_ref[e]))
        row_weight = [jnp.maximum(1.0 - jnp.abs(flow[0] - s), 0.0) for s in range(-2, 3)]
        col_weight = [jnp.maximum(1.0 - jnp.abs(flow[1] - s), 0.0) for s in range(-2, 3)]
        mine = pair * 2 + k
        for e in range(2):
            value = flow[e]
            for rs in range(5):
                inner = None
                for cs in range(5):
                    term = col_weight[cs] * bands[k, e, rs, cs]
                    inner = term if inner is None else inner + term
                value = value + row_weight[rs] * inner
            every[mine, e] = value
        copy = pltpu.make_async_remote_copy(
            src_ref=every.at[mine],
            dst_ref=every.at[mine],
            send_sem=cand_send.at[k],
            recv_sem=cand_recv.at[k],
            device_id=(partner, row, col),
            device_id_type=MESH,
        )
        copy.start()
        if k == 0:
            first_copy = copy
        else:
            second_copy = copy

    first_copy.wait()
    second_copy.wait()
    for number in range(5):
        only_if(sends_to[number], image_copies[number].wait_send)
        only_if(sends_to[number], prior_copies[number].wait_send)


def vote(every, cand_ref, vote_ref):
    pair = lax.axis_index("pair")
    for k in range(2):
        cand_ref[k] = every[2 * pair + k]
    c = [[every[k, e] for e in range(2)] for k in range(4)]
    score = [None] * 4
    for i in range(4):
        for j in range(i + 1, 4):
            dr = c[i][0] - c[j][0]
            dc = c[i][1] - c[j][1]
            apart = dr * dr + dc * dc
            score[i] = apart if score[i] is None else score[i] + apart
            score[j] = apart if score[j] is None else score[j] + apart
    weight = [jnp.exp(score[i] * (-1.0 / (3 * sharpness))) for i in range(4)]
    bottom = (weight[0] + weight[1]) + (weight[2] + weight[3])
    for e in range(2):
        top = (weight[0] * c[0][e] + weight[1] * c[1][e]) + (
            weight[2] * c[2][e] + weight[3] * c[3][e]
        )
        vote_ref[e] = top / bottom


def solution(mesh):
    n_rows = mesh.shape["rows"]
    in_specs = (
        P("rows", "cols"),
        P("pair", "rows", "cols"),
        P("pair", None, "rows", "cols"),
        P("pair"),
        P(),
        P(),
        P(),
        P(),
        P(),
        P(),
        P(),
    )
    out_specs = (P("pair", None, "rows", "cols"), P(None, "rows", "cols"))
    vmem = pl.BlockSpec(memory_space=pltpu.VMEM)
    hbm = pl.BlockSpec(memory_space=pltpu.HBM)
    dma = pltpu.SemaphoreType.DMA

    def shards(*args):
        args = [pltpu.with_memory_space_constraint(x, pltpu.HBM) for x in args]
        every = pl.pallas_call(
            functools.partial(kernel, n_rows),
            out_shape=pltpu.VMEM((4, 2, 8, 256), F32),
            in_specs=[hbm] * 11,
            out_specs=vmem,
            scratch_shapes=[
                pltpu.SMEM((2,), jnp.int32),
                pltpu.VMEM((3, 128), BF),
                pltpu.VMEM((9, 2, 128), BF),
                pltpu.VMEM((128,), F32),
                pltpu.VMEM((2, 128), F32),
                pltpu.VMEM((9, 2, 128), BF),
                pltpu.SMEM((2,), F32),
                pltpu.VMEM((3, 32, RING), BF),
                pltpu.VMEM((32, 128), BF),
                pltpu.VMEM((8, 256), BF),
                pltpu.VMEM((2, 8, 256), BF),
                pltpu.VMEM((2, 2, 24, RING), F32),
                pltpu.VMEM((2, 3, 2, 256, 256), BF),
                pltpu.VMEM((RING + 8, 128), F32),
                pltpu.VMEM((2, RING, 128), F32),
                pltpu.VMEM((6, 32, 128), F32),
                pltpu.VMEM((128, 14 * 128), BF),
                pltpu.VMEM((6, 24, 128), F32),
                pltpu.VMEM((5, 256, 128), BF),
                pltpu.VMEM((2, 7, ROWS_X, 256), BF),
                pltpu.VMEM((2, 6, ROWS_X, 256), BF),
                pltpu.VMEM((2, 2, ROWS_M, 256), F32),
                pltpu.VMEM((2, 2, ROWS_M, 256), F32),
                pltpu.VMEM((2, ROWS_M, 128), F32),
                pltpu.VMEM((2, 5, ROWS_M, 256), BF),
                pltpu.VMEM((2, 2, 5, 5, 8, 256), F32),
                pltpu.VMEM((3, 7 * Q, 256), F32),
                dma((9,)),
                dma((6,)),
                dma,
                dma((5,)),
                dma((5,)),
                dma((5,)),
                dma((5,)),
                dma((2,)),
                dma((2,)),
            ],
            compiler_params=pltpu.CompilerParams(
                collective_id=0, has_side_effects=True, vmem_limit_bytes=40 * 1024 * 1024
            ),
        )(*args)
        return pl.pallas_call(
            vote,
            out_shape=(
                jax.ShapeDtypeStruct((2, 2, 8, 256), F32),
                jax.ShapeDtypeStruct((2, 8, 256), F32),
            ),
            in_specs=[vmem],
            out_specs=(vmem, vmem),
        )(pltpu.with_memory_space_constraint(every, pltpu.VMEM))

    return jax.shard_map(shards, mesh=mesh, in_specs=in_specs, out_specs=out_specs, check_vma=False)
```

time: 26.3 us -> 19 us (0.72)
  the two profiles are of different devices: /device:TPU:1 before, /device:TPU:128 now
where the time goes in v3:
time: 19 us; the launch traced here: 18.9 us
  Pallas kernels  18.3 us (96%)
  between operations  0.64 us (3%)
    pallas_call x1, Pallas kernels, shards(): pl.pallas_call(functools.partial(kernel, n_rows), out_shape=pltpu.VMEM((4...  17.6 us
    pallas_call x1, Pallas kernels, shards(): pl.pallas_call(vote, out_shape=(jax.ShapeDtypeStruct((2, 2, 8, 256), F32)...  0.64 us

profile of v3, /device:TPU:128, one launch (start us, length us, event | category | flops | bytes accessed | tf_op | source)
XLA Modules:
  0.0 18.9 jit_solution(15739936015276026050)
XLA Ops:
  0.6 17.6 %shard_map.122.every = f32[4,2,8,256]{3,2,1,0:T(8,128)S(1)} custom-call(bf16[8,256]{1,0:T(8,128)(2,1)} %src_in.1, bf16[2,8,256]{2,1,0:T(8,128)(2,1)} %tgt_in.1, f32[2,2,8,256]{3,2,1,0:T(8,128)} %prior_ref.1, s32[2]{0:T(128)} %off_in.1, bf16[3,128]{1,0:T(4,128)(2,1)} %table_in.1, bf16[9,2,128]{2,1,0:T(2,128)(2,1)} %inw_in.1, f32[128]{0:T(128)} %inb_in.1, ...), custom_call_target="tpu_custom_call" | custom-call | tf_op jit(solution)/shard_map/pallas_call | solution.py:479
  18.3 0.6 %shard_map.123 = (f32[2,2,8,256]{3,2,1,0:T(8,128)}, f32[2,8,256]{2,1,0:T(8,128)}) custom-call(f32[4,2,8,256]{3,2,1,0:T(8,128)S(1)} %shard_map.122.every), custom_call_target="tpu_custom_call" | custom-call | tf_op jit(solution)/shard_map/pallas_call | solution.py:526

commit v4 on v3

--- a/solution.py
+++ b/solution.py
@@ -26,11 +26,12 @@
     return lax.dot_general(a, b, (dims, ((), ())), preferred_element_type=F32)
 
 
-def store_slabs(ref, index, y):
-    ref[index, 0:ROWS_M, :] = y.astype(BF)
-    first = pltpu.roll(y[0:Q], Q - 1, 0)
-    second = pltpu.roll(y[Q : 2 * Q], Q - 1, 0)
-    ref[index, ROWS_M:ROWS_X, :] = jnp.concatenate([first, second], axis=0).astype(BF)
+def store_slabs(ref, index, y, low=0):
+    ref[index, low : low + y.shape[0], :] = y.astype(BF)
+    if low == 0:
+        first = pltpu.roll(y[0:Q], Q - 1, 0)
+        second = pltpu.roll(y[Q : 2 * Q], Q - 1, 0)
+        ref[index, ROWS_M:ROWS_X, :] = jnp.concatenate([first, second], axis=0).astype(BF)
 
 
 def kernel(
@@ -71,6 +72,7 @@
     part1,
     part2,
     sums_out,
+    own_lhs,
     part_of,
     bands,
     masks,
@@ -162,81 +164,8 @@
     ).astype(BF)
     img[0, :, 0:256] = own
     side[...] = jnp.where(col == 0, own[:, 128:256], own[:, 0:128])
-    order[...] = jnp.zeros_like(order)
-
-    m_slab = lax.broadcasted_iota(jnp.int32, (7, Q, 256), 0)
-    m_chunk = lax.broadcasted_iota(jnp.int32, (7, Q, 256), 1)
-    m_at = m_chunk * STRIDE + m_slab + col * 256
-    for layer in range(3):
-        inside = (m_at >= 3 - layer) & (m_at < 512 + 3 - layer)
-        masks[layer] = jnp.where(inside, 1.0, 0.0).reshape(7 * Q, 256)
-
     for copy in loads[2:]:
         copy.wait()
-    gin[...] = jnp.zeros_like(gin)
-    for b in range(3):
-        for ch in range(2):
-            for a in range(3):
-                w = inw_ref[3 * a + b, ch : ch + 1, :].astype(F32)
-                gin[2 * b + ch, a : a + 1, :] = w
-                gin[2 * b + ch, 16 + a : 17 + a, :] = w
-    for r in range(14):
-        start = (20 - r) % 16
-        block = jnp.concatenate(
-            [gin[g, start : start + 16, :] for g in range(6)] + [jnp.zeros((32, 128), F32)], axis=0
-        )
-        toe[:, r * 128 : (r + 1) * 128] = block.astype(BF)
-
-    gout[...] = jnp.zeros_like(gout)
-    for b in range(3):
-        for e in range(2):
-            for a in range(3):
-                gout[2 * b + e, 10 - a : 11 - a, :] = outw_ref[3 * a + b, e : e + 1, :].astype(F32)
-    for p in range(5):
-        for h in range(2):
-            start = 10 - (2 * p + h)
-            block = jnp.concatenate(
-                [gout[g, start : start + 8, :] for g in range(6)] + [jnp.zeros((80, 128), F32)], axis=0
-            )
-            wout[p, h * 128 : (h + 1) * 128, :] = jnp.transpose(block).astype(BF)
-
-    for layer in range(2):
-        for b in range(3):
-            wts[layer, b, 0, 0:128, 128:256] = jnp.zeros((128, 128), BF)
-            wts[layer, b, 1, 128:256, 0:128] = jnp.zeros((128, 128), BF)
-
-    pl.semaphore_wait(barrier, 2 + 2 * has_up.astype(jnp.int32) + 2 * has_down.astype(jnp.int32))
-
-    main = pl.ds(0, 256)
-    edge = pl.ds(256, 128)
-    half = pl.ds(pl.multiple_of((1 - col) * 128, 128), 128)
-    routes = ((2, main), (1, main), (0, edge), (2, edge), (1, edge))
-    image_copies = [None] * 5
-    for number in (0, 3, 1, 4, 2):
-        slot, lanes = routes[number]
-        copy = pltpu.make_async_remote_copy(
-            src_ref=img.at[0, :, main] if number < 2 else side,
-            dst_ref=img.at[slot, :, lanes],
-            send_sem=img_send.at[number],
-            recv_sem=img_recv.at[number],
-            device_id=places[number],
-            device_id_type=MESH,
-        )
-        only_if(sends_to[number], copy.start)
-        image_copies[number] = copy
-    prior_copies = []
-    for number, (slot, lanes) in enumerate(routes):
-        start = (8, 0, 16)[slot]
-        copy = pltpu.make_async_remote_copy(
-            src_ref=prior_ref if number < 2 else prior_ref.at[:, :, :, half],
-            dst_ref=pri.at[:, :, pl.ds(start, 8), lanes],
-            send_sem=pri_send.at[number],
-            recv_sem=pri_recv.at[number],
-            device_id=places[number],
-            device_id_type=MESH,
-        )
-        only_if(sends_to[number], copy.start)
-        prior_copies.append(copy)
 
     lane8 = lax.broadcasted_iota(jnp.int32, (8, RING), 1)
     sub8 = lax.broadcasted_iota(jnp.int32, (8, RING), 0)
@@ -274,10 +203,18 @@
     def own_image(s):
         return (jnp.where(lanes_ok, image(0, s), 0.0), blank)
 
+    def own_image_alone(s):
+        mine = img[0, :, 0:256].astype(F32)[8 * s : 8 * s + 8]
+        return (jnp.concatenate([mine, jnp.zeros((8, 128), F32)], axis=1), blank)
+
+    def above_rows(s):
+        return (blank, jnp.where(jnp.logical_and(sub8 >= 4, above_ok), image(1, s), 0.0))
+
+    def below_rows(s):
+        return (blank, jnp.where(jnp.logical_and(sub8 < 4, below_ok), image(2, s), 0.0))
+
     def halo_rows(s):
-        above = jnp.where(above_ok, image(1, s), 0.0)
-        below = jnp.where(below_ok, image(2, s), 0.0)
-        return (blank, jnp.where(sub8 < 4, below, above))
+        return (blank, jnp.where(sub8 < 4, below_rows(s)[1], above_rows(s)[1]))
 
     def row_bias(bias, first_row):
         which = first_row + lax.broadcasted_iota(jnp.int32, (1, 256), 1) // 128
@@ -286,41 +223,45 @@
     def twice(vector):
         return jnp.concatenate([vector, vector], axis=1)
 
-    def finish(total, bias, layer):
+    def finish(total, bias, layer, low=0):
         y = jnp.maximum(total + bias, 0.0)
-        return jnp.concatenate([y[0 : 7 * Q] * masks[layer], y[7 * Q :]], axis=0)
+        if low > 0:
+            return y
+        count = min(7 * Q, y.shape[0])
+        masked = y[0:count] * masks[layer, 0:count, :]
+        return masked if count == y.shape[0] else jnp.concatenate([masked, y[count:]], axis=0)
 
     def first_layer(k, p, lhs):
         total = dot(lhs, toe[:, p * 256 : (p + 1) * 256])
         bias_here = row_bias(first_bias[k], row * tile_rows + 2 * p - 3)
         store_slabs(feat.at[k], p, finish(total, bias_here, 0))
 
-    def taps(source, k, p, layer, wheres):
+    def taps(source, k, p, layer, wheres, low, count):
         total = None
         for where in wheres:
             for b in range(3):
-                term = dot(source[k, p + where, b * Q : b * Q + ROWS_M, :], wts[layer, b, where])
+                rows = source[k, p + where, b * Q + low : b * Q + low + count, :]
+                term = dot(rows, wts[layer, b, where])
                 total = term if total is None else total + term
         return total
 
     hidden_layers = ((feat, part1), (hid1, part2))
 
-    def hidden(k, p, layer, wheres=(0, 1), part=None):
+    def hidden(k, p, layer, wheres=(0, 1), part=None, low=0, count=ROWS_M):
         source, sums = hidden_layers[layer]
-        total = taps(source, k, p, layer, wheres)
+        total = taps(source, k, p, layer, wheres, low, count)
         if part is not None:
             total = total + sums[k, part]
         bias_here = row_bias(hidden_bias[layer], row * tile_rows + 2 * p - 2 + layer)
-        y = finish(total, bias_here, layer + 1)
+        y = finish(total, bias_here, layer + 1, low)
         if layer == 0:
-            store_slabs(hid1.at[k], p, y)
-            return None
-        part_of[k, p] = y.astype(BF)
-        return None
-
-    def partial(k, p, layer, where, part):
+            store_slabs(hid1.at[k], p, y, low)
+        else:
+            part_of[k, p, low : low + count, :] = y.astype(BF)
+
+    def partial(k, p, layer, where, part, low=0, count=ROWS_M):
         source, sums = hidden_layers[layer]
-        sums[k, part] = taps(source, k, p, layer, (where,))
+        sums[k, part, low : low + count, :] = taps(source, k, p, layer, (where,), low, count)
 
     table = table_ref[...].astype(F32)
     in_bias = inb_ref[...].reshape(1, 128)
@@ -332,52 +273,186 @@
             embed = embed + jnp.where(off_ref[k] == o, table[o : o + 1], 0.0)
         first_bias.append(twice(in_bias + embed))
 
-    image_copies[2].wait_recv()
-    lhs_own = gather_columns(own_image)
-    for k in range(2):
-        for p in (2, 3, 4):
-            first_layer(k, p, lhs_own[k])
-    for copy in weight_copies:
-        copy.wait()
-    for k in range(2):
-        for p in (2, 3):
-            hidden(k, p, 0)
-    for k in range(2):
-        partial(k, 1, 0, 1, 0)
-        partial(k, 4, 0, 0, 1)
-    for k in range(2):
-        hidden(k, 2, 1)
-    for k in range(2):
-        partial(k, 1, 1, 1, 0)
-        partial(k, 3, 1, 0, 1)
-    for k in range(2):
-        sums_out[k] = dot(part_of[k, 2], wout[2])
-
-    for number in (0, 1, 3, 4):
-        only_if(comes_from[number], image_copies[number].wait_recv)
-    lhs = [a + b for a, b in zip(lhs_own, gather_columns(halo_rows))]
-    for k in range(2):
-        for p in (0, 1, 5, 6):
-            first_layer(k, p, lhs[k])
-    for k in range(2):
-        hidden(k, 0, 0)
-        hidden(k, 1, 0, (0,), 0)
-        hidden(k, 4, 0, (1,), 1)
-        hidden(k, 5, 0)
+    main = pl.ds(0, 256)
+    edge = pl.ds(256, 128)
+    half = pl.ds(pl.multiple_of((1 - col) * 128, 128), 128)
+    routes = ((2, main), (1, main), (0, edge), (2, edge), (1, edge))
+    prior_copies = []
+    for number, (slot, lanes) in enumerate(routes):
+        start = (8, 0, 16)[slot]
+        copy = pltpu.make_async_remote_copy(
+            src_ref=prior_ref if number < 2 else prior_ref.at[:, :, :, half],
+            dst_ref=pri.at[:, :, pl.ds(start, 8), lanes],
+            send_sem=pri_send.at[number],
+            recv_sem=pri_recv.at[number],
+            device_id=places[number],
+            device_id_type=MESH,
+        )
+        prior_copies.append(copy)
+
+    def send_priors():
+        for number in range(5):
+            only_if(sends_to[number], prior_copies[number].start)
+
+    def make_constants():
+        order[...] = jnp.zeros_like(order)
+
+        m_slab = lax.broadcasted_iota(jnp.int32, (7, Q, 256), 0)
+        m_chunk = lax.broadcasted_iota(jnp.int32, (7, Q, 256), 1)
+        m_at = m_chunk * STRIDE + m_slab + col * 256
+        for layer in range(3):
+            inside = (m_at >= 3 - layer) & (m_at < 512 + 3 - layer)
+            masks[layer] = jnp.where(inside, 1.0, 0.0).reshape(7 * Q, 256)
+
+        gin[...] = jnp.zeros_like(gin)
+        for b in range(3):
+            for ch in range(2):
+                for a in range(3):
+                    w = inw_ref[3 * a + b, ch : ch + 1, :].astype(F32)
+                    gin[2 * b + ch, a : a + 1, :] = w
+                    gin[2 * b + ch, 16 + a : 17 + a, :] = w
+        for r in range(14):
+            start = (20 - r) % 16
+            block = jnp.concatenate(
+                [gin[g, start : start + 16, :] for g in range(6)] + [jnp.zeros((32, 128), F32)], axis=0
+            )
+            toe[:, r * 128 : (r + 1) * 128] = block.astype(BF)
+
+        gout[...] = jnp.zeros_like(gout)
+        for b in range(3):
+            for e in range(2):
+                for a in range(3):
+                    gout[2 * b + e, 10 - a : 11 - a, :] = outw_ref[3 * a + b, e : e + 1, :].astype(F32)
+        for p in range(5):
+            for h in range(2):
+                start = 10 - (2 * p + h)
+                block = jnp.concatenate(
+                    [gout[g, start : start + 8, :] for g in range(6)] + [jnp.zeros((80, 128), F32)], axis=0
+                )
+                wout[p, h * 128 : (h + 1) * 128, :] = jnp.transpose(block).astype(BF)
+
+        for layer in range(2):
+            for b in range(3):
+                wts[layer, b, 0, 0:128, 128:256] = jnp.zeros((128, 128), BF)
+                wts[layer, b, 1, 128:256, 0:128] = jnp.zeros((128, 128), BF)
+
+
+    def own_first(rows_of):
+        columns = gather_columns(rows_of)
+        for k in range(2):
+            own_lhs[k] = columns[k]
+            for p in (2, 3, 4):
+                first_layer(k, p, columns[k])
+
+    def own_hidden(first_ranges, second_ranges):
+        for low, count in first_ranges:
+            for k in range(2):
+                for p in (2, 3):
+                    hidden(k, p, 0, low=low, count=count)
+            for k in range(2):
+                partial(k, 1, 0, 1, 0, low, count)
+                partial(k, 4, 0, 0, 1, low, count)
+        for low, count in second_ranges:
+            for k in range(2):
+                hidden(k, 2, 1, low=low, count=count)
+            for k in range(2):
+                partial(k, 1, 1, 1, 0, low, count)
+                partial(k, 3, 1, 0, 1, low, count)
+        for low, count in second_ranges:
+            for k in range(2):
+                sums_out[k, low : low + count, :] = dot(part_of[k, 2, low : low + count, :], wout[2])
+
+    def wait_weights():
+        for copy in weight_copies:
+            copy.wait()
+
+    whole = ((0, ROWS_M),)
+    early = jnp.logical_and(row % 8 == 0, jnp.logical_and(row != 0, row != n_rows // 2))
+
+    @pl.when(early)
+    def _():
+        make_constants()
+        own_first(own_image_alone)
+        wait_weights()
+        own_hidden(whole, whole)
+
+    pl.semaphore_wait(barrier, 2 + 2 * has_up.astype(jnp.int32) + 2 * has_down.astype(jnp.int32))
+
+    image_copies = [None] * 5
+    for number in (2, 0, 3, 1, 4):
+        slot, lanes = routes[number]
+        copy = pltpu.make_async_remote_copy(
+            src_ref=img.at[0, :, main] if number < 2 else side,
+            dst_ref=img.at[slot, :, lanes],
+            send_sem=img_send.at[number],
+            recv_sem=img_recv.at[number],
+            device_id=places[number],
+            device_id_type=MESH,
+        )
+        only_if(sends_to[number], copy.start)
+        image_copies[number] = copy
+
+    @pl.when(early)
+    def _():
+        send_priors()
+        image_copies[2].wait_recv()
+        own_first(own_image)
+        own_hidden(((0, 5 * Q),), ((0, 4 * Q), (16 * Q, Q)))
+
+    @pl.when(jnp.logical_not(early))
+    def _():
+        make_constants()
+        image_copies[2].wait_recv()
+        own_first(own_image)
+        send_priors()
+        wait_weights()
+        own_hidden(whole, whole)
+
+    def outer(rows_of, sides, arrivals):
+        for number in arrivals:
+            only_if(comes_from[number], image_copies[number].wait_recv)
+        more = gather_columns(rows_of)
+        for k in range(2):
+            lhs = own_lhs[k] + more[k]
+            for side_of in sides:
+                for p in ((0, 1), (5, 6))[side_of]:
+                    first_layer(k, p, lhs)
+        for k in range(2):
+            for side_of in sides:
+                hidden(k, (0, 5)[side_of], 0)
+                hidden(k, (1, 4)[side_of], 0, (side_of,), side_of)
+        for k in range(2):
+            for side_of in sides:
+                hidden(k, (0, 4)[side_of], 1)
+                hidden(k, (1, 3)[side_of], 1, (side_of,), side_of)
+        for k in range(2):
+            total = sums_out[k]
+            for side_of in sides:
+                for p in ((0, 1), (4, 3))[side_of]:
+                    total = total + dot(part_of[k, p], wout[p])
+            sums_out[k] = total
+
+    middle = n_rows // 2
+    below_first = jnp.logical_or(row == middle, jnp.logical_and(row % 8 == 1, row > 1))
+    above_first = row == middle - 1
+
+    @pl.when(below_first)
+    def _():
+        outer(below_rows, (1,), (0, 3))
+        outer(above_rows, (0,), (1, 4))
+
+    @pl.when(above_first)
+    def _():
+        outer(above_rows, (0,), (1, 4))
+        outer(below_rows, (1,), (0, 3))
+
+    @pl.when(jnp.logical_not(jnp.logical_or(below_first, above_first)))
+    def _():
+        outer(halo_rows, (0, 1), (0, 1, 3, 4))
+
     for number in range(5):
         only_if(comes_from[number], prior_copies[number].wait_recv)
     own_prior.wait()
-    for k in range(2):
-        hidden(k, 0, 1)
-        hidden(k, 1, 1, (0,), 0)
-        hidden(k, 3, 1, (1,), 1)
-        hidden(k, 4, 1)
-    flat = []
-    for k in range(2):
-        total = sums_out[k]
-        for p in (0, 1, 3, 4):
-            total = total + dot(part_of[k, p], wout[p])
-        flat.append(total)
     for k in range(2):
         for e in range(2):
             pri[k, e, 0:8, :] = jnp.where(above_ok, pri[k, e, 0:8, :], 0.0)
@@ -391,7 +466,7 @@
 
     for k in range(2):
         for i in range(STRIDE):
-            order[k, pl.ds(i, Q, STRIDE), :] = flat[k][i * Q : (i + 1) * Q]
+            order[k, pl.ds(i, Q, STRIDE), :] = sums_out[k, i * Q : (i + 1) * Q, :]
         natural = jnp.transpose(order[k])
         flow = []
         for e in range(2):
@@ -506,6 +581,7 @@
                 pltpu.VMEM((2, 2, ROWS_M, 256), F32),
                 pltpu.VMEM((2, 2, ROWS_M, 256), F32),
                 pltpu.VMEM((2, ROWS_M, 128), F32),
+                pltpu.VMEM((2, ROWS_M, 128), BF),
                 pltpu.VMEM((2, 5, ROWS_M, 256), BF),
                 pltpu.VMEM((2, 2, 5, 5, 8, 256), F32),
                 pltpu.VMEM((3, 7 * Q, 256), F32),

time: 19 us -> 18.5 us (0.974)
  Pallas kernels: 18.3 us -> 17.7 us
    pallas_call x1, Pallas kernels: 17.6 us -> 17 us  [shards(): pl.pallas_call(functools.partial(kernel, n_rows), out_shape=pltpu.VMEM((4...]
where the time goes in v4:
time: 18.5 us; the launch traced here: 18.3 us
  Pallas kernels  17.7 us (96%)
  between operations  0.64 us (3%)
    pallas_call x1, Pallas kernels, shards(): pl.pallas_call(functools.partial(kernel, n_rows), out_shape=pltpu.VMEM((4...  17 us
    pallas_call x1, Pallas kernels, shards(): pl.pallas_call(vote, out_shape=(jax.ShapeDtypeStruct((2, 2, 8, 256), F32)...  0.64 us

profile of v4, /device:TPU:128, one launch (start us, length us, event | category | flops | bytes accessed | tf_op | source)
XLA Modules:
  0.0 18.3 jit_solution(9934526116860260262)
XLA Ops:
  0.6 17.0 %shard_map.122.every = f32[4,2,8,256]{3,2,1,0:T(8,128)S(1)} custom-call(bf16[8,256]{1,0:T(8,128)(2,1)} %src_in.1, bf16[2,8,256]{2,1,0:T(8,128)(2,1)} %tgt_in.1, f32[2,2,8,256]{3,2,1,0:T(8,128)} %prior_ref.1, s32[2]{0:T(128)} %off_in.1, bf16[3,128]{1,0:T(4,128)(2,1)} %table_in.1, bf16[9,2,128]{2,1,0:T(2,128)(2,1)} %inw_in.1, f32[128]{0:T(128)} %inb_in.1, ...), custom_call_target="tpu_custom_call" | custom-call | tf_op jit(solution)/shard_map/pallas_call | solution.py:554
  17.7 0.6 %shard_map.123 = (f32[2,2,8,256]{3,2,1,0:T(8,128)}, f32[2,8,256]{2,1,0:T(8,128)}) custom-call(f32[4,2,8,256]{3,2,1,0:T(8,128)S(1)} %shard_map.122.every), custom_call_target="tpu_custom_call" | custom-call | tf_op jit(solution)/shard_map/pallas_call | solution.py:602

commit v5 on v4

--- a/solution.py
+++ b/solution.py
@@ -408,7 +408,22 @@
         wait_weights()
         own_hidden(whole, whole)
 
-    def outer(rows_of, sides, arrivals):
+    def shift_priors():
+        for number in range(5):
+            only_if(comes_from[number], prior_copies[number].wait_recv)
+        own_prior.wait()
+        for k in range(2):
+            for e in range(2):
+                pri[k, e, 0:8, :] = jnp.where(above_ok, pri[k, e, 0:8, :], 0.0)
+                pri[k, e, 8:16, :] = jnp.where(lanes_ok, pri[k, e, 8:16, :], 0.0)
+                pri[k, e, 16:24, :] = jnp.where(below_ok, pri[k, e, 16:24, :], 0.0)
+                for rs in range(5):
+                    band = pri[k, e, 6 + rs : 14 + rs, :]
+                    for cs in range(5):
+                        moved = band if cs == 2 else pltpu.roll(band, (RING + 2 - cs) % RING, 1)
+                        bands[k, e, rs, cs] = moved[:, 0:256]
+
+    def outer(rows_of, sides, arrivals, then=None):
         for number in arrivals:
             only_if(comes_from[number], image_copies[number].wait_recv)
         more = gather_columns(rows_of)
@@ -421,6 +436,8 @@
             for side_of in sides:
                 hidden(k, (0, 5)[side_of], 0)
                 hidden(k, (1, 4)[side_of], 0, (side_of,), side_of)
+        if then is not None:
+            then()
         for k in range(2):
             for side_of in sides:
                 hidden(k, (0, 4)[side_of], 1)
@@ -439,30 +456,16 @@
     @pl.when(below_first)
     def _():
         outer(below_rows, (1,), (0, 3))
-        outer(above_rows, (0,), (1, 4))
+        outer(above_rows, (0,), (1, 4), shift_priors)
 
     @pl.when(above_first)
     def _():
         outer(above_rows, (0,), (1, 4))
-        outer(below_rows, (1,), (0, 3))
+        outer(below_rows, (1,), (0, 3), shift_priors)
 
     @pl.when(jnp.logical_not(jnp.logical_or(below_first, above_first)))
     def _():
-        outer(halo_rows, (0, 1), (0, 1, 3, 4))
-
-    for number in range(5):
-        only_if(comes_from[number], prior_copies[number].wait_recv)
-    own_prior.wait()
-    for k in range(2):
-        for e in range(2):
-            pri[k, e, 0:8, :] = jnp.where(above_ok, pri[k, e, 0:8, :], 0.0)
-            pri[k, e, 8:16, :] = jnp.where(lanes_ok, pri[k, e, 8:16, :], 0.0)
-            pri[k, e, 16:24, :] = jnp.where(below_ok, pri[k, e, 16:24, :], 0.0)
-            for rs in range(5):
-                band = pri[k, e, 6 + rs : 14 + rs, :]
-                for cs in range(5):
-                    moved = band if cs == 2 else pltpu.roll(band, (RING + 2 - cs) % RING, 1)
-                    bands[k, e, rs, cs] = moved[:, 0:256]
+        outer(halo_rows, (0, 1), (0, 1, 3, 4), shift_priors)
 
     for k in range(2):
         for i in range(STRIDE):

time: 18.5 us -> 18.5 us (level)
  no operation moved by 1% of the time
where the time goes in v5:
time: 18.5 us; the launch traced here: 18.3 us
  Pallas kernels  17.7 us (96%)
  between operations  0.64 us (3%)
    pallas_call x1, Pallas kernels, shards(): pl.pallas_call(functools.partial(kernel, n_rows), out_shape=pltpu.VMEM((4...  17.1 us
    pallas_call x1, Pallas kernels, shards(): pl.pallas_call(vote, out_shape=(jax.ShapeDtypeStruct((2, 2, 8, 256), F32)...  0.64 us

profile of v5, /device:TPU:128, one launch (start us, length us, event | category | flops | bytes accessed | tf_op | source)
XLA Modules:
  0.0 18.3 jit_solution(16002602445719557057)
XLA Ops:
  0.6 17.1 %shard_map.122.every = f32[4,2,8,256]{3,2,1,0:T(8,128)S(1)} custom-call(bf16[8,256]{1,0:T(8,128)(2,1)} %src_in.1, bf16[2,8,256]{2,1,0:T(8,128)(2,1)} %tgt_in.1, f32[2,2,8,256]{3,2,1,0:T(8,128)} %prior_ref.1, s32[2]{0:T(128)} %off_in.1, bf16[3,128]{1,0:T(4,128)(2,1)} %table_in.1, bf16[9,2,128]{2,1,0:T(2,128)(2,1)} %inw_in.1, f32[128]{0:T(128)} %inb_in.1, ...), custom_call_target="tpu_custom_call" | custom-call | tf_op jit(solution)/shard_map/pallas_call | solution.py:557
  17.7 0.6 %shard_map.123 = (f32[2,2,8,256]{3,2,1,0:T(8,128)}, f32[2,8,256]{2,1,0:T(8,128)}) custom-call(f32[4,2,8,256]{3,2,1,0:T(8,128)S(1)} %shard_map.122.every), custom_call_target="tpu_custom_call" | custom-call | tf_op jit(solution)/shard_map/pallas_call | solution.py:605
